TPU v7x, 32 devices: a whole 2x2x4 slice. The times are simulated.
32 devices in a mesh: seq: 16 (over z, y, x), tp: 2 (over core).
Axes of the slice: x: 2, y: 2, z: 4, core: 2. Of those that a mesh axis runs over, the one named last changes fastest.
Arguments:
- tokens: bfloat16 [24576, 768], P('seq'), may hold values from -6 to 6
- short_lengths: int32 [16, 3], P('seq'), may hold values from 1 to 512, 1024 in all within a row
- query_weight: bfloat16 [768, 768], P(None, 'tp'), may hold values from -0.21875 to 0.21875
- key_weight: bfloat16 [768, 768], P(None, 'tp'), may hold values from -0.21875 to 0.21875
- value_weight: bfloat16 [768, 768], P(None, 'tp'), may hold values from -0.21875 to 0.21875
- conv_kernel: float32 [12, 33], P('tp'), may hold values from -0.3 to 0.3
- out_weight: bfloat16 [768, 768], P('tp'), may hold values from -0.625 to 0.625
- gain_one: float32 [768], replicated, may hold values from 0.5 to 1.5
- bias_one: float32 [768], replicated, may hold values from -1 to 1
- inner_weight: bfloat16 [768, 3072], P(None, 'tp'), may hold values from -0.21875 to 0.21875
- outer_weight: bfloat16 [3072, 768], P('tp'), may hold values from -0.109375 to 0.109375
- gain_two: float32 [768], replicated, may hold values from 0.5 to 1.5
- bias_two: float32 [768], replicated, may hold values from -1 to 1
- cotangent: bfloat16 [24576, 768], P('seq'), may hold values from -6 to 6
Outputs:
- output: bfloat16 [24576, 768], P('seq')
- token_grad: float32 [24576, 768], P('seq')
- query_grad: float32 [768, 768], P(None, 'tp')
- key_grad: float32 [768, 768], P(None, 'tp')
- value_grad: float32 [768, 768], P(None, 'tp')
- kernel_grad: float32 [12, 33], P('tp')
- out_grad: float32 [768, 768], P('tp')
- gain_one_grad: float32 [768], replicated
- bias_one_grad: float32 [768], replicated
- inner_grad: float32 [768, 3072], P(None, 'tp')
- outer_grad: float32 [3072, 768], P('tp')
- gain_two_grad: float32 [768], replicated
- bias_two_grad: float32 [768], replicated
Inputs may be any that keep to these rules, and one draw needn't show every extreme that they name: `short_lengths`: row d lists the lengths of device d's short items in order; they sum to 1024, and the largest of each row is exactly 512.
All inputs are finite; a program needn't handle non-finite values.
Results may differ from a plain program's by a relative error of at most 0.013.
Values may be sent and summed in bfloat16 or wider, within the bound.
No kernel may reach another device: no remote copies, remote signals or barrier semaphores. Data moves between devices by JAX's collectives and lax.ppermute only.
A program may use at most 320 MiB of HBM per device.

v0:
```python
import math

import jax
import jax.numpy as jnp
from jax import lax
from jax.sharding import PartitionSpec as P

TAU = 8
CONV_WIDTH = 33
HALF_WIDTH = 16
GROUP = 16
PIECE = 256


COS_SCALE = 0.98
EPS_UNIT = 1e-06
EPS_NORM = 1e-05


def passed_along(x, axis, by):
    peers = lax.axis_size(axis)
    pairs = [(i, i + by) for i in range(peers) if 0 <= i + by < peers]
    return lax.ppermute(x, axis, pairs)


def padded_2(block, sides, width):
    for axis, dim in sides:
        count = lax.axis_size(axis)
        forward = [(i, i + 1) for i in range(count - 1)]
        backward = [(target, source) for source, target in forward]
        low = lax.ppermute(
            lax.slice_in_dim(block, block.shape[dim] - width, None, axis=dim), axis, forward
        )
        high = lax.ppermute(lax.slice_in_dim(block, 0, width, axis=dim), axis, backward)
        block = jnp.concatenate([low, block, high], axis=dim)
    return block


def unit_rows(values):
    return values * lax.rsqrt(jnp.sum(values * values, axis=-1, keepdims=True) + EPS_UNIT)


def layer_norm(values, gain, bias):
    row_mean = jnp.mean(values, axis=-1, keepdims=True)
    centered = values - row_mean
    variance = jnp.mean(centered * centered, axis=-1, keepdims=True)
    return centered * lax.rsqrt(variance + EPS_NORM) * gain + bias


def exact_gelu(values):
    return jax.nn.gelu(values, approximate=False)


def closeness(cosine):
    return 1.0 - jnp.arccos(cosine) / math.pi


def collision_slope(cosine, grad_weights):
    nearness = closeness(cosine)
    return (
        grad_weights * (TAU * nearness ** (TAU - 1)) / (math.pi * jnp.sqrt(1.0 - cosine * cosine))
    )


def contract_rows(left, right):
    return lax.dot_general(
        left, right, (((0,), (0,)), ((), ())), preferred_element_type=jnp.float32
    )


def contract_features(left, right):
    return lax.dot_general(
        left, right, (((1,), (1,)), ((), ())), preferred_element_type=jnp.float32
    )


def tap_sum(padded, kernel, masks, length):
    running = jnp.zeros(padded[:length].shape, jnp.float32)
    for tap_index in range(kernel.shape[1]):
        window = padded[tap_index : tap_index + length] * kernel[:, tap_index][:, None]
        if masks is not None:
            window = window * masks[tap_index]
        running = running + window
    return running


def tap_products(grad_rows, padded, masks, length, axes):
    columns = []
    for tap_index in range(CONV_WIDTH):
        window = grad_rows * padded[tap_index : tap_index + length]
        if masks is not None:
            window = window * masks[tap_index]
        columns.append(jnp.sum(window, axis=axes))
    return jnp.stack(columns, axis=1)


def shards(
    tokens,
    short_lengths,
    query_weight,
    key_weight,
    value_weight,
    conv_kernel,
    out_weight,
    gain_one,
    bias_one,
    inner_weight,
    outer_weight,
    gain_two,
    bias_two,
    cotangent,
):
    row_total = tokens.shape[0]
    heads_dev = conv_kernel.shape[0]
    head_cols = query_weight.shape[1]
    head_dim = head_cols // heads_dev
    long_rows = 2 * PIECE
    short_rows = row_total - long_rows
    block_rows = math.gcd(short_rows, 512)
    block_count = short_rows // block_rows
    local_place = lax.axis_index("seq") % GROUP
    group_first = local_place == 0
    group_last = local_place == GROUP - 1

    def rotate(packed):
        from_prev = passed_along(packed, "seq", 1)
        from_last = passed_along(packed, "seq", -(GROUP - 1))
        return jnp.where(group_first, from_last, from_prev)

    def clip_rim(padded):
        lower = jnp.where(group_first, jnp.zeros_like(padded[:HALF_WIDTH]), padded[:HALF_WIDTH])
        upper = jnp.where(group_last, jnp.zeros_like(padded[-HALF_WIDTH:]), padded[-HALF_WIDTH:])
        return jnp.concatenate([lower, padded[HALF_WIDTH:-HALF_WIDTH], upper], axis=0)

    item_ends = jnp.cumsum(short_lengths[0])
    positions = jnp.arange(short_rows, dtype=jnp.int32)
    item_ids = jnp.sum((positions[:, None] >= item_ends[None, :]).astype(jnp.int32), axis=1)
    padded_ids = jnp.pad(item_ids, (HALF_WIDTH, HALF_WIDTH), constant_values=-1)
    short_masks = [
        (padded_ids[tap_index : tap_index + short_rows] == item_ids).astype(jnp.float32)[
            :, None, None
        ]
        for tap_index in range(CONV_WIDTH)
    ]
    query_rows = jnp.dot(tokens, query_weight, preferred_element_type=jnp.float32).reshape(
        row_total, heads_dev, head_dim
    )
    key_rows = jnp.dot(tokens, key_weight, preferred_element_type=jnp.float32).reshape(
        row_total, heads_dev, head_dim
    )
    value_low = (
        jnp.dot(tokens, value_weight, preferred_element_type=jnp.float32)
        .astype(jnp.bfloat16)
        .reshape(row_total, heads_dev, head_dim)
    )
    query_unit, query_unit_back = jax.vjp(unit_rows, query_rows)
    key_unit, key_unit_back = jax.vjp(unit_rows, key_rows)
    query_low = query_unit.astype(jnp.bfloat16)
    key_low = key_unit.astype(jnp.bfloat16)

    def split_heads(row_block):
        return row_block.reshape(-1, 2, heads_dev, head_dim)

    long_query = split_heads(query_low[:long_rows])
    long_key_heads = split_heads(key_low[:long_rows])
    long_value_heads = split_heads(value_low[:long_rows])
    long_value = long_value_heads.reshape(PIECE, 2, head_cols)
    long_pack = jnp.concatenate(
        [key_low[:long_rows].reshape(PIECE, 2, head_cols), long_value], axis=2
    )

    def first_half(packed):
        return split_heads(packed[:, :, :head_cols])

    def second_half(packed):
        return split_heads(packed[:, :, head_cols:])

    def pair_cosine(query_part, key_part):
        return COS_SCALE * jnp.einsum(
            "aihe,bihe->ihab", query_part, key_part, preferred_element_type=jnp.float32
        )

    def attend_pack(running, packed):
        weights_low = (closeness(pair_cosine(long_query, first_half(packed))) ** TAU).astype(
            jnp.bfloat16
        )
        return running + jnp.einsum(
            "ihab,bihe->aihe", weights_low, second_half(packed), preferred_element_type=jnp.float32
        )

    def forward_turn(step, carry):
        packed = rotate(carry[1])
        return (attend_pack(carry[0], packed), packed)

    long_zero = jnp.zeros((PIECE, 2, heads_dev, head_dim), jnp.float32)
    long_att, _ = lax.fori_loop(
        0, GROUP - 1, forward_turn, (attend_pack(long_zero, long_pack), long_pack)
    )
    value_rim = clip_rim(padded_2(long_value, (("seq", 0),), HALF_WIDTH))
    value_rim_heads = split_heads(value_rim)
    long_total = long_att + tap_sum(value_rim_heads, conv_kernel, None, PIECE)
    short_query = query_low[long_rows:]
    short_key = key_low[long_rows:]
    short_value = value_low[long_rows:]
    query_blocks = short_query.reshape(block_count, block_rows, heads_dev, head_dim)
    id_blocks = item_ids.reshape(block_count, block_rows)

    def short_cosine(query_block, id_block):
        cosine = COS_SCALE * jnp.einsum(
            "qhe,khe->hqk", query_block, short_key, preferred_element_type=jnp.float32
        )
        same_item = (id_block[:, None] == item_ids[None, :]).astype(jnp.float32)[None]
        return (cosine, same_item)

    def attend_short(packed):
        cosine, same_item = short_cosine(packed[0], packed[1])
        weights_low = (closeness(cosine) ** TAU * same_item).astype(jnp.bfloat16)
        return jnp.einsum(
            "hqk,khe->qhe", weights_low, short_value, preferred_element_type=jnp.float32
        )

    short_att = lax.map(attend_short, (query_blocks, id_blocks)).reshape(
        short_rows, heads_dev, head_dim
    )
    value_pad = jnp.pad(short_value, ((HALF_WIDTH, HALF_WIDTH), (0, 0), (0, 0)))
    short_total = short_att + tap_sum(value_pad, conv_kernel, short_masks, short_rows)
    attention = jnp.concatenate(
        [long_total.reshape(long_rows, head_cols), short_total.reshape(short_rows, head_cols)],
        axis=0,
    )
    mixed_low = attention.astype(jnp.bfloat16)
    projected = lax.psum(jnp.dot(mixed_low, out_weight, preferred_element_type=jnp.float32), "tp")
    hidden = tokens.astype(jnp.float32) + projected
    normed, norm_one_back = jax.vjp(layer_norm, hidden, gain_one, bias_one)
    normed_low = normed.astype(jnp.bfloat16)
    pre_act = jnp.dot(normed_low, inner_weight, preferred_element_type=jnp.float32)
    act_rows, gelu_back = jax.vjp(exact_gelu, pre_act)
    act_low = act_rows.astype(jnp.bfloat16)
    ffn_out = lax.psum(jnp.dot(act_low, outer_weight, preferred_element_type=jnp.float32), "tp")
    output, norm_two_back = jax.vjp(layer_norm, normed + ffn_out, gain_two, bias_two)
    grad_sum, gain_two_grad, bias_two_grad = norm_two_back(cotangent.astype(jnp.float32))
    grad_ffn_low = grad_sum.astype(jnp.bfloat16)
    outer_grad = contract_rows(act_low, grad_ffn_low)
    grad_pre_low = gelu_back(contract_features(grad_ffn_low, outer_weight))[0].astype(jnp.bfloat16)
    inner_grad = contract_rows(normed_low, grad_pre_low)
    grad_normed = grad_sum + lax.psum(contract_features(grad_pre_low, inner_weight), "tp")
    grad_hidden, gain_one_grad, bias_one_grad = norm_one_back(grad_normed)
    grad_proj_low = grad_hidden.astype(jnp.bfloat16)
    out_grad = contract_rows(mixed_low, grad_proj_low)
    grad_att_low = contract_features(grad_proj_low, out_weight).astype(jnp.bfloat16)
    grad_long_low = grad_att_low[:long_rows].reshape(PIECE, 2, head_cols)
    grad_long = split_heads(grad_long_low)
    grad_short = grad_att_low[long_rows:].reshape(short_rows, heads_dev, head_dim)
    flipped = conv_kernel[:, ::-1]
    grad_rim = clip_rim(padded_2(grad_long_low, (("seq", 0),), HALF_WIDTH))
    conv_value_long = tap_sum(split_heads(grad_rim), flipped, None, PIECE)
    grad_pad = jnp.pad(grad_short, ((HALF_WIDTH, HALF_WIDTH), (0, 0), (0, 0)))
    conv_value_short = tap_sum(grad_pad, flipped, short_masks, short_rows)
    kernel_grad = tap_products(
        grad_long.astype(jnp.float32), value_rim_heads, None, PIECE, (0, 1, 3)
    ) + tap_products(grad_short.astype(jnp.float32), value_pad, short_masks, short_rows, (0, 2))

    def pair_terms(query_part, grad_part, key_part, value_part):
        cosine = pair_cosine(query_part, key_part)
        weights_low = (closeness(cosine) ** TAU).astype(jnp.bfloat16)
        grad_weights = jnp.einsum(
            "aihe,bihe->ihab", grad_part, value_part, preferred_element_type=jnp.float32
        )
        return (weights_low, collision_slope(cosine, grad_weights).astype(jnp.bfloat16))

    query_pack = jnp.concatenate(
        [query_low[:long_rows].reshape(PIECE, 2, head_cols), grad_long_low], axis=2
    )

    def query_side(running, packed):
        key_part = first_half(packed)
        weights_low, slope_low = pair_terms(long_query, grad_long, key_part, second_half(packed))
        return running + COS_SCALE * jnp.einsum(
            "ihab,bihe->aihe", slope_low, key_part, preferred_element_type=jnp.float32
        )

    def key_side(running, packed):
        query_part = first_half(packed)
        grad_part = second_half(packed)
        weights_low, slope_low = pair_terms(query_part, grad_part, long_key_heads, long_value_heads)
        key_total = running[0] + COS_SCALE * jnp.einsum(
            "ihab,aihe->bihe", slope_low, query_part, preferred_element_type=jnp.float32
        )
        value_total = running[1] + jnp.einsum(
            "ihab,aihe->bihe", weights_low, grad_part, preferred_element_type=jnp.float32
        )
        return (key_total, value_total)

    def backward_turn(step, carry):
        key_packed = rotate(carry[2])
        query_packed = rotate(carry[3])
        return (
            query_side(carry[0], key_packed),
            key_side(carry[1], query_packed),
            key_packed,
            query_packed,
        )

    start = (
        query_side(long_zero, long_pack),
        key_side((long_zero, long_zero), query_pack),
        long_pack,
        query_pack,
    )
    query_grad_long, key_sums, _, _ = lax.fori_loop(0, GROUP - 1, backward_turn, start)
    key_grad_long, value_att_long = key_sums
    grad_blocks = grad_short.reshape(block_count, block_rows, heads_dev, head_dim)

    def short_back(running, packed):
        query_block, grad_block, id_block = packed
        cosine, same_item = short_cosine(query_block, id_block)
        grad_weights = jnp.einsum(
            "qhe,khe->hqk", grad_block, short_value, preferred_element_type=jnp.float32
        )
        weights_low = (closeness(cosine) ** TAU * same_item).astype(jnp.bfloat16)
        slope_low = (collision_slope(cosine, grad_weights) * same_item).astype(jnp.bfloat16)
        query_grad_block = COS_SCALE * jnp.einsum(
            "hqk,khe->qhe", slope_low, short_key, preferred_element_type=jnp.float32
        )
        key_total = running[0] + COS_SCALE * jnp.einsum(
            "hqk,qhe->khe", slope_low, query_block, preferred_element_type=jnp.float32
        )
        value_total = running[1] + jnp.einsum(
            "hqk,qhe->khe", weights_low, grad_block, preferred_element_type=jnp.float32
        )
        return ((key_total, value_total), query_grad_block)

    short_zero = jnp.zeros((short_rows, heads_dev, head_dim), jnp.float32)
    short_sums, query_grad_short = lax.scan(
        short_back, (short_zero, short_zero), (query_blocks, grad_blocks, id_blocks)
    )
    key_grad_short, value_att_short = short_sums
    query_unit_grad = jnp.concatenate(
        [
            query_grad_long.reshape(long_rows, heads_dev, head_dim),
            query_grad_short.reshape(short_rows, heads_dev, head_dim),
        ],
        axis=0,
    )
    key_unit_grad = jnp.concatenate(
        [key_grad_long.reshape(long_rows, heads_dev, head_dim), key_grad_short], axis=0
    )
    value_grad_rows = jnp.concatenate(
        [
            (value_att_long + conv_value_long).reshape(long_rows, head_cols),
            (value_att_short + conv_value_short).reshape(short_rows, head_cols),
        ],
        axis=0,
    )
    grad_query_low = (
        query_unit_back(query_unit_grad)[0].reshape(row_total, head_cols).astype(jnp.bfloat16)
    )
    grad_key_low = (
        key_unit_back(key_unit_grad)[0].reshape(row_total, head_cols).astype(jnp.bfloat16)
    )
    grad_value_low = value_grad_rows.astype(jnp.bfloat16)
    query_grad = contract_rows(tokens, grad_query_low)
    key_grad = contract_rows(tokens, grad_key_low)
    value_grad = contract_rows(tokens, grad_value_low)
    token_part = (
        contract_features(grad_query_low, query_weight)
        + contract_features(grad_key_low, key_weight)
        + contract_features(grad_value_low, value_weight)
    )
    token_grad = grad_hidden + lax.psum(token_part.astype(jnp.bfloat16), "tp").astype(jnp.float32)
    summed = lax.psum(
        (
            query_grad,
            key_grad,
            value_grad,
            kernel_grad,
            out_grad,
            gain_one_grad,
            bias_one_grad,
            inner_grad,
            outer_grad,
            gain_two_grad,
            bias_two_grad,
        ),
        "seq",
    )
    return (
        output.astype(jnp.bfloat16),
        token_grad,
        summed[0],
        summed[1],
        summed[2],
        summed[3],
        summed[4],
        summed[5],
        summed[6],
        summed[7],
        summed[8],
        summed[9],
        summed[10],
    )


def solution(mesh):
    placed = (
        P("seq", None),
        P("seq", None),
        P(None, "tp"),
        P(None, "tp"),
        P(None, "tp"),
        P("tp", None),
        P("tp", None),
        P(),
        P(),
        P(None, "tp"),
        P("tp", None),
        P(),
        P(),
        P("seq", None),
    )
    return jax.shard_map(
        shards,
        mesh=mesh,
        in_specs=placed,
        out_specs=(
            P("seq", None),
            P("seq", None),
            P(None, "tp"),
            P(None, "tp"),
            P(None, "tp"),
            P("tp", None),
            P("tp", None),
            P(),
            P(),
            P(None, "tp"),
            P("tp", None),
            P(),
            P(),
        ),
        check_vma=False,
    )
```

profile of v0, /device:TPU:0, one launch (start us, length us, event | category | flops | bytes accessed | tf_op | source)
XLA Modules:
  0.0 2798.7 jit_solution(453987743431576716)
XLA Ops:
  64.4 129.7 %while.56 = (s32[]{:T(128)}, f32[2,512,6,64]{1,0,3,2:T(2,128)}, bf16[2,512,6,64]{1,3,2,0:T(8,128)(2,1)}, bf16[1024,6,64]{0,2,1:T(8,128)(2,1)S(1)}, s32[2,512]{1,...) while((s32[]{:T(128)}, f32[2,512,6,64]{1,0,3,2:T(2,128)}, ...), condition=%wide.region_7.8_spmd, body=%wide.region_6.7_spmd.sunk | while | flops 840957952 | bytes 10103397 | solution.py:222
  86.7 31.8 %fusion.555 = f32[1,512,6,64]{1,3,2,0:T(8,128)} fusion(bf16[1024,6,64]{0,2,1:T(8,128)(2,1)} %get-tuple-element.1091, f32[512,1024]{1,0:T(8,128)} %compare_convert_fusion.4, bf16[1024,6,64]{0,2,1:T(8,128)(2,1)S(1)} %get-tuple-element.1088, bf16[2,512,6,64]{1,3,2,0:T(8,128)(2,1)} %get-tuple-element.1087, s32[]{:T(128)} %get-tuple-element.1076), kind=kOutput, calls=%fused_computation.22.clone.1 | convolution fusion | flops 839909376 | bytes 4850176 | tf_op jit(solution)/shard_map/while/body/eval_jaxpr/hqk,khe->qhe/dot_general | solution.py:218
  121.3 15.0 dynamic_update_slice.10
  137.8 31.8 %fusion.555 = f32[1,512,6,64]{1,3,2,0:T(8,128)} fusion(bf16[1024,6,64]{0,2,1:T(8,128)(2,1)} %get-tuple-element.1091, f32[512,1024]{1,0:T(8,128)} %compare_convert_fusion.4, bf16[1024,6,64]{0,2,1:T(8,128)(2,1)S(1)} %get-tuple-element.1088, bf16[2,512,6,64]{1,3,2,0:T(8,128)(2,1)} %get-tuple-element.1087, s32[]{:T(128)} %get-tuple-element.1076), kind=kOutput, calls=%fused_computation.22.clone.1 | convolution fusion | flops 839909376 | bytes 4850176 | tf_op jit(solution)/shard_map/while/body/eval_jaxpr/hqk,khe->qhe/dot_general | solution.py:218
  172.4 15.0 dynamic_update_slice.10
  209.9 14.3 fusion.167
  307.9 467.3 %while.55 = (s32[]{:T(128)}, f32[256,2,6,64]{0,3,2,1:T(8,128)}, bf16[256,2,768]{0,2,1:T(8,128)(2,1)S(1)}, pred[]{:T(512)}, bf16[256,2,6,64]{0,3,2,1:T(8,128)(2,1)}, /*index=5*/s32[]{:T(128)}) while((s32[]{:T(128)}, f32[256,2,6,64]{0,3,2,1:T(8,128)}, bf16[256,2,768]{0,2,1:T(8,128)(2,1)S(1)}, pred[]{:T(512)}, bf16[256,2,6,64]{0,3,2,1:T(8,128)(2,1)}, ...), condition=%wide.region_3.4_spmd, body=%wide.region_2.3_spmd.sunk | while | flops 209780736 | bytes 12976278 | solution.py:196
  315.7 17.3 collective-permute-done
  349.4 18.7 collective-permute-done
  383.2 19.3 collective-permute-done
  417.5 18.3 collective-permute-done
  450.8 17.4 collective-permute-done
  483.2 16.5 collective-permute-done
  514.7 15.6 collective-permute-done
  545.3 14.6 collective-permute-done
  575.0 14.1 collective-permute-done
  604.1 14.1 collective-permute-done
  633.2 14.1 collective-permute-done
  662.3 14.1 collective-permute-done
  691.4 14.1 collective-permute-done
  720.5 14.1 collective-permute-done
  749.7 14.1 collective-permute-done
  796.5 29.8 %all-reduce.11.cloned.1.call-done = f32[1536,768]{1,0:T(8,128)} async-done(((f32[1536,768]{1,0:T(8,128)}), f32[1536,768]{1,0:T(8,128)}) %all-reduce.11.cloned.1.call-update) | async-done | bytes 4718608 | tf_op jit(solution)/shard_map/psum | solution.py:232
  832.2 25.1 multiply_convert_fusion.14
  865.0 30.4 %all-reduce.13.cloned.1.call-done = f32[1536,768]{1,0:T(8,128)} async-done(((f32[1536,768]{1,0:T(8,128)}), f32[1536,768]{1,0:T(8,128)}) %all-reduce.13.cloned.1.call-update) | async-done | bytes 4718608 | tf_op jit(solution)/shard_map/psum | solution.py:239
  908.2 13.5 add_convert_fusion
  943.4 17.1 all-reduce.15.cloned.1.call-done
  994.2 982.8 %while.57 = (s32[]{:T(128)}, f32[256,2,6,64]{0,3,2,1:T(8,128)}, f32[256,2,6,64]{0,3,2,1:T(8,128)}, f32[256,2,6,64]{0,3,2,1:T(8,128)}, bf16[256,2,768]{0,2,1:T(8,...) while((s32[]{:T(128)}, f32[256,2,6,64]{0,3,2,1:T(8,128)}, ...), condition=%wide.region_20.21_spmd, body=%wide.region_19.20_spmd.sunk | while | flops 741015552 | bytes 87687616 | solution.py:310
  1022.4 15.7 collective-permute-done.2
  1064.9 12.0 fusion.571
  1092.8 15.8 collective-permute-done.2
  1135.4 12.0 fusion.571
  1163.3 15.8 collective-permute-done.2
  1206.0 12.0 fusion.571
  1233.9 12.1 collective-permute-done.2
  1272.8 12.0 fusion.571
  1334.8 12.0 fusion.571
  1896.0 12.0 fusion.571
  2001.8 181.1 %while.58 = (s32[]{:T(128)}, f32[1024,6,64]{0,2,1:T(8,128)S(1)}, f32[1024,6,64]{0,2,1:T(8,128)}, f32[2,512,6,64]{1,0,3,2:T(2,128)}, bf16[2,512,6,64]{1,3,2,0:T(8...) while((s32[]{:T(128)}, f32[1024,6,64]{0,2,1:T(8,128)S(1)}, ...), condition=%wide.region_22.23_spmd.clone, body=%wide.region_21.22_spmd.clone.sunk | while | flops 2107703296 | bytes 217591632 | solution.py:334
  2006.5 32.5 %fusion.583 = bf16[6,512,1024]{2,1,0:T(8,128)(2,1)S(1)} fusion(f32[6,512,1024]{2,1,0:T(8,128)S(1)} %fusion.582, f32[512,1024]{1,0:T(8,128)S(1)} %compare_convert_fusion.5, bf16[1024,6,64]{0,2,1:T(8,128)(2,1)S(1)} %get-tuple-element.1142, bf16[2,512,6,64]{1,3,2,0:T(8,128)(2,1)S(1)} %copy-done.102, s32[]{:T(128)} %get-tuple-element.1124), kind=kOutput, calls=%fused_computation.88.clone.1 | convolution fusion | flops 459276288 | bytes 22151172 | tf_op jit(solution)/shard_map/while/body/eval_jaxpr/qhe,khe->hqk/dot_general | solution.py:317
  2042.6 15.0 dynamic_update_slice.11
  2064.0 28.2 %bitcast_add_fusion.7 = f32[1024,6,64]{0,2,1:T(8,128)} fusion(f32[1024,6,64]{0,2,1:T(8,128)} %get-tuple-element.1126, f32[6,512,1024]{2,1,0:T(8,128)S(1)} %copy-done.4, f32[512,1024]{1,0:T(8,128)} %copy-done.13, pred[]{:T(512)S(6)} %compare.7, bf16[2,512,6,64]{1,3,2,0:T(8,128)(2,1)} %get-tuple-element.1141, s32[]{:T(128)} %get-tuple-element.1124), kind=kOutput, calls=%fused_computation.91.clone.1 | convolution fusion | flops 438042624 | bytes 18219520 | tf_op jit(solution)/shard_map/while/body/eval_jaxpr/hqk,qhe->khe/dot_general | solution.py:328
  2096.8 32.6 %fusion.583 = bf16[6,512,1024]{2,1,0:T(8,128)(2,1)S(1)} fusion(f32[6,512,1024]{2,1,0:T(8,128)S(1)} %fusion.582, f32[512,1024]{1,0:T(8,128)S(1)} %compare_convert_fusion.5, bf16[1024,6,64]{0,2,1:T(8,128)(2,1)S(1)} %get-tuple-element.1142, bf16[2,512,6,64]{1,3,2,0:T(8,128)(2,1)S(1)} %copy-done.102, s32[]{:T(128)} %get-tuple-element.1124), kind=kOutput, calls=%fused_computation.88.clone.1 | convolution fusion | flops 459276288 | bytes 22151172 | tf_op jit(solution)/shard_map/while/body/eval_jaxpr/qhe,khe->hqk/dot_general | solution.py:317
  2132.8 15.0 dynamic_update_slice.11
  2154.2 28.3 %bitcast_add_fusion.7 = f32[1024,6,64]{0,2,1:T(8,128)} fusion(f32[1024,6,64]{0,2,1:T(8,128)} %get-tuple-element.1126, f32[6,512,1024]{2,1,0:T(8,128)S(1)} %copy-done.4, f32[512,1024]{1,0:T(8,128)} %copy-done.13, pred[]{:T(512)S(6)} %compare.7, bf16[2,512,6,64]{1,3,2,0:T(8,128)(2,1)} %get-tuple-element.1141, s32[]{:T(128)} %get-tuple-element.1124), kind=kOutput, calls=%fused_computation.91.clone.1 | convolution fusion | flops 438042624 | bytes 18219520 | tf_op jit(solution)/shard_map/while/body/eval_jaxpr/hqk,qhe->khe/dot_general | solution.py:328
  2208.7 14.6 fusion.257
  2454.4 85.6 %all-reduce.3 = (f32[6,33]{1,0:T(8,128)}, f32[768]{0:T(1024)}, f32[768]{0:T(1024)}, f32[768]{0:T(1024)}, f32[768]{0:T(1024)}) all-reduce(f32[6,33]{1,0:T(8,128)S(1)} %add.690, f32[768]{0:T(1024)S(1)} %copy-done.219, f32[768]{0:T(1024)S(1)} %copy-done.220, f32[768]{0:T(1024)S(1)} %copy-done.217, ...), channel_id=1, replica_groups=mesh['seq'=16,'tp'=2] {'seq'}, use_global_device_ids=true, to_apply=%region_129.130 | all-reduce | flops 3270 | bytes 26160 | tf_op jit(solution)/shard_map/psum | solution.py:371
  2545.8 230.5 %all-reduce.19.cloned.1.call-done = (f32[768,384]{0,1:T(8,128)}, f32[768,384]{0,1:T(8,128)}, f32[768,384]{0,1:T(8,128)}, f32[384,768]{1,0:T(8,128)}, f32[768,1536]{1,0:T(8,128)}, /*index=5*/f32[1536,768]{1,0:T(8,128)}) async-done(((f32[768,384]{0,1:T(8,128)}, f32[768,384]{0,1:T(8,128)}, f32[768,384]{0,1:T(8,128)}, f32[384,768]{1,0:T(8,128)}, f32[768,1536]{1,0:T(8,128)}, /*index=5*/f32[1536,768]{1,0:T(8,128)}), ...) | async-done | bytes 14155792 | tf_op jit(solution)/shard_map/psum | solution.py:371
  (1515 shorter events, 1659.3 us)
Async XLA Ops:
  7.2 819.1 %all-reduce.11.cloned.1.call-start = ((), (), s32[]{:S(2)}) async-start(), calls=%async_computation | async-start | bytes 9437184 | tf_op jit(solution)/shard_map/psum | solution.py:232
  14.0 214.1 %collective-permute-start.6 = (bf16[16,2,384]{2,0,1:T(8,128)(2,1)}, bf16[16,2,384]{2,0,1:T(8,128)(2,1)}, u32[]{:S(2)}, u32[]{:S(2)}) collective-permute-start(bf16[16,2,384]{2,0,1:T(8,128)(2,1)} %copy.1067), channel_id=1, source_target_pairs={{0,2},{2,4},{4,6},{6,8},{8,10},{10,12},{12,14},{14,16},{16,18},{18... | collective-permute-start | bytes 73736 | tf_op jit(solution)/shard_map/ppermute | solution.py:31
  22.1 207.4 %collective-permute-start.7 = (bf16[16,2,384]{2,0,1:T(8,128)(2,1)}, bf16[16,2,384]{2,0,1:T(8,128)(2,1)}, u32[]{:S(2)}, u32[]{:S(2)}) collective-permute-start(bf16[16,2,384]{2,0,1:T(8,128)(2,1)} %copy.1086), channel_id=1, source_target_pairs={{2,0},{4,2},{6,4},{8,6},{10,8},{12,10},{14,12},{16,14},{18,16},{20... | collective-permute-start | bytes 73736 | tf_op jit(solution)/shard_map/ppermute | solution.py:34
  308.0 25.0 collective-permute-start
  309.3 23.7 collective-permute-start.1
  344.5 23.7 collective-permute-start
  796.5 98.9 %all-reduce.13.cloned.1.call-start = ((), (), s32[]{:S(2)}) async-start(), calls=%async_computation.1 | async-start | bytes 9437184 | tf_op jit(solution)/shard_map/psum | solution.py:239
  864.9 95.6 %all-reduce.15.cloned.1.call-start = ((), (), s32[]{:S(2)}) async-start(), calls=%async_computation.2 | async-start | bytes 9437184 | tf_op jit(solution)/shard_map/psum | solution.py:246
  930.1 1609.9 %all-reduce.17.cloned.1.call-start = ((), (), s32[]{:S(2)}) async-start(), calls=%async_computation.3 | async-start | bytes 4718592 | tf_op jit(solution)/shard_map/psum | solution.py:370
  1012.1 26.0 collective-permute-start.2
  1013.4 24.7 collective-permute-start.3
  1018.3 37.9 %collective-permute-start.4 = (bf16[256,2,768]{0,2,1:T(8,128)(2,1)S(1)}, bf16[256,2,768]{0,2,1:T(8,128)(2,1)S(1)}, u32[]{:S(2)}, u32[]{:S(2)}) collective-permute-start(bf16[256,2,768]{0,2,1:T(8,128)(2,1)S(1)} %get-tuple-element.1165), channel_id=1, source_target_pairs={{30,0},{31,1}} | collective-permute-start | bytes 2359304 | tf_op jit(solution)/shard_map/while/body/eval_jaxpr/ppermute | solution.py:23
  1019.6 36.6 %collective-permute-start.5 = (bf16[256,2,768]{0,2,1:T(8,128)(2,1)S(1)}, bf16[256,2,768]{0,2,1:T(8,128)(2,1)}, u32[]{:S(2)}, u32[]{:S(2)}) collective-permute-start(bf16[256,2,768]{0,2,1:T(8,128)(2,1)S(1)} %get-tuple-element.1165), channel_id=1, source_target_pairs={{0,2},{2,4},{4,6},{6,8},{8,10},{10,12},{12,14},{14,16},{16,18},{18... | collective-permute-start | bytes 2359304 | tf_op jit(solution)/shard_map/while/body/eval_jaxpr/ppermute | solution.py:23
  1082.6 26.1 collective-permute-start.2
  1083.9 24.8 collective-permute-start.3
  1087.8 38.9 %collective-permute-start.4 = (bf16[256,2,768]{0,2,1:T(8,128)(2,1)S(1)}, bf16[256,2,768]{0,2,1:T(8,128)(2,1)S(1)}, u32[]{:S(2)}, u32[]{:S(2)}) collective-permute-start(bf16[256,2,768]{0,2,1:T(8,128)(2,1)S(1)} %get-tuple-element.1165), channel_id=1, source_target_pairs={{30,0},{31,1}} | collective-permute-start | bytes 2359304 | tf_op jit(solution)/shard_map/while/body/eval_jaxpr/ppermute | solution.py:23
  1089.1 37.6 %collective-permute-start.5 = (bf16[256,2,768]{0,2,1:T(8,128)(2,1)S(1)}, bf16[256,2,768]{0,2,1:T(8,128)(2,1)}, u32[]{:S(2)}, u32[]{:S(2)}) collective-permute-start(bf16[256,2,768]{0,2,1:T(8,128)(2,1)S(1)} %get-tuple-element.1165), channel_id=1, source_target_pairs={{0,2},{2,4},{4,6},{6,8},{8,10},{10,12},{12,14},{14,16},{16,18},{18... | collective-permute-start | bytes 2359304 | tf_op jit(solution)/shard_map/while/body/eval_jaxpr/ppermute | solution.py:23
  1153.1 26.1 collective-permute-start.2
  1154.4 24.8 collective-permute-start.3
  1157.4 39.8 %collective-permute-start.4 = (bf16[256,2,768]{0,2,1:T(8,128)(2,1)S(1)}, bf16[256,2,768]{0,2,1:T(8,128)(2,1)S(1)}, u32[]{:S(2)}, u32[]{:S(2)}) collective-permute-start(bf16[256,2,768]{0,2,1:T(8,128)(2,1)S(1)} %get-tuple-element.1165), channel_id=1, source_target_pairs={{30,0},{31,1}} | collective-permute-start | bytes 2359304 | tf_op jit(solution)/shard_map/while/body/eval_jaxpr/ppermute | solution.py:23
  1158.7 38.5 %collective-permute-start.5 = (bf16[256,2,768]{0,2,1:T(8,128)(2,1)S(1)}, bf16[256,2,768]{0,2,1:T(8,128)(2,1)}, u32[]{:S(2)}, u32[]{:S(2)}) collective-permute-start(bf16[256,2,768]{0,2,1:T(8,128)(2,1)S(1)} %get-tuple-element.1165), channel_id=1, source_target_pairs={{0,2},{2,4},{4,6},{6,8},{8,10},{10,12},{12,14},{14,16},{16,18},{18... | collective-permute-start | bytes 2359304 | tf_op jit(solution)/shard_map/while/body/eval_jaxpr/ppermute | solution.py:23
  1227.8 36.3 %collective-permute-start.4 = (bf16[256,2,768]{0,2,1:T(8,128)(2,1)S(1)}, bf16[256,2,768]{0,2,1:T(8,128)(2,1)S(1)}, u32[]{:S(2)}, u32[]{:S(2)}) collective-permute-start(bf16[256,2,768]{0,2,1:T(8,128)(2,1)S(1)} %get-tuple-element.1165), channel_id=1, source_target_pairs={{30,0},{31,1}} | collective-permute-start | bytes 2359304 | tf_op jit(solution)/shard_map/while/body/eval_jaxpr/ppermute | solution.py:23
  1229.1 35.0 %collective-permute-start.5 = (bf16[256,2,768]{0,2,1:T(8,128)(2,1)S(1)}, bf16[256,2,768]{0,2,1:T(8,128)(2,1)}, u32[]{:S(2)}, u32[]{:S(2)}) collective-permute-start(bf16[256,2,768]{0,2,1:T(8,128)(2,1)S(1)} %get-tuple-element.1165), channel_id=1, source_target_pairs={{0,2},{2,4},{4,6},{6,8},{8,10},{10,12},{12,14},{14,16},{16,18},{18... | collective-permute-start | bytes 2359304 | tf_op jit(solution)/shard_map/while/body/eval_jaxpr/ppermute | solution.py:23
  1295.3 30.8 %collective-permute-start.4 = (bf16[256,2,768]{0,2,1:T(8,128)(2,1)S(1)}, bf16[256,2,768]{0,2,1:T(8,128)(2,1)S(1)}, u32[]{:S(2)}, u32[]{:S(2)}) collective-permute-start(bf16[256,2,768]{0,2,1:T(8,128)(2,1)S(1)} %get-tuple-element.1165), channel_id=1, source_target_pairs={{30,0},{31,1}} | collective-permute-start | bytes 2359304 | tf_op jit(solution)/shard_map/while/body/eval_jaxpr/ppermute | solution.py:23
  1296.6 29.5 %collective-permute-start.5 = (bf16[256,2,768]{0,2,1:T(8,128)(2,1)S(1)}, bf16[256,2,768]{0,2,1:T(8,128)(2,1)}, u32[]{:S(2)}, u32[]{:S(2)}) collective-permute-start(bf16[256,2,768]{0,2,1:T(8,128)(2,1)S(1)} %get-tuple-element.1165), channel_id=1, source_target_pairs={{0,2},{2,4},{4,6},{6,8},{8,10},{10,12},{12,14},{14,16},{16,18},{18... | collective-permute-start | bytes 2359304 | tf_op jit(solution)/shard_map/while/body/eval_jaxpr/ppermute | solution.py:23
  1357.4 30.7 %collective-permute-start.4 = (bf16[256,2,768]{0,2,1:T(8,128)(2,1)S(1)}, bf16[256,2,768]{0,2,1:T(8,128)(2,1)S(1)}, u32[]{:S(2)}, u32[]{:S(2)}) collective-permute-start(bf16[256,2,768]{0,2,1:T(8,128)(2,1)S(1)} %get-tuple-element.1165), channel_id=1, source_target_pairs={{30,0},{31,1}} | collective-permute-start | bytes 2359304 | tf_op jit(solution)/shard_map/while/body/eval_jaxpr/ppermute | solution.py:23
  1358.6 29.4 %collective-permute-start.5 = (bf16[256,2,768]{0,2,1:T(8,128)(2,1)S(1)}, bf16[256,2,768]{0,2,1:T(8,128)(2,1)}, u32[]{:S(2)}, u32[]{:S(2)}) collective-permute-start(bf16[256,2,768]{0,2,1:T(8,128)(2,1)S(1)} %get-tuple-element.1165), channel_id=1, source_target_pairs={{0,2},{2,4},{4,6},{6,8},{8,10},{10,12},{12,14},{14,16},{16,18},{18... | collective-permute-start | bytes 2359304 | tf_op jit(solution)/shard_map/while/body/eval_jaxpr/ppermute | solution.py:23
  1419.4 30.7 %collective-permute-start.4 = (bf16[256,2,768]{0,2,1:T(8,128)(2,1)S(1)}, bf16[256,2,768]{0,2,1:T(8,128)(2,1)S(1)}, u32[]{:S(2)}, u32[]{:S(2)}) collective-permute-start(bf16[256,2,768]{0,2,1:T(8,128)(2,1)S(1)} %get-tuple-element.1165), channel_id=1, source_target_pairs={{30,0},{31,1}} | collective-permute-start | bytes 2359304 | tf_op jit(solution)/shard_map/while/body/eval_jaxpr/ppermute | solution.py:23
  1420.7 29.4 %collective-permute-start.5 = (bf16[256,2,768]{0,2,1:T(8,128)(2,1)S(1)}, bf16[256,2,768]{0,2,1:T(8,128)(2,1)}, u32[]{:S(2)}, u32[]{:S(2)}) collective-permute-start(bf16[256,2,768]{0,2,1:T(8,128)(2,1)S(1)} %get-tuple-element.1165), channel_id=1, source_target_pairs={{0,2},{2,4},{4,6},{6,8},{8,10},{10,12},{12,14},{14,16},{16,18},{18... | collective-permute-start | bytes 2359304 | tf_op jit(solution)/shard_map/while/body/eval_jaxpr/ppermute | solution.py:23
  1481.4 30.7 %collective-permute-start.4 = (bf16[256,2,768]{0,2,1:T(8,128)(2,1)S(1)}, bf16[256,2,768]{0,2,1:T(8,128)(2,1)S(1)}, u32[]{:S(2)}, u32[]{:S(2)}) collective-permute-start(bf16[256,2,768]{0,2,1:T(8,128)(2,1)S(1)} %get-tuple-element.1165), channel_id=1, source_target_pairs={{30,0},{31,1}} | collective-permute-start | bytes 2359304 | tf_op jit(solution)/shard_map/while/body/eval_jaxpr/ppermute | solution.py:23
  1482.7 29.4 %collective-permute-start.5 = (bf16[256,2,768]{0,2,1:T(8,128)(2,1)S(1)}, bf16[256,2,768]{0,2,1:T(8,128)(2,1)}, u32[]{:S(2)}, u32[]{:S(2)}) collective-permute-start(bf16[256,2,768]{0,2,1:T(8,128)(2,1)S(1)} %get-tuple-element.1165), channel_id=1, source_target_pairs={{0,2},{2,4},{4,6},{6,8},{8,10},{10,12},{12,14},{14,16},{16,18},{18... | collective-permute-start | bytes 2359304 | tf_op jit(solution)/shard_map/while/body/eval_jaxpr/ppermute | solution.py:23
  1544.0 30.2 %collective-permute-start.4 = (bf16[256,2,768]{0,2,1:T(8,128)(2,1)S(1)}, bf16[256,2,768]{0,2,1:T(8,128)(2,1)S(1)}, u32[]{:S(2)}, u32[]{:S(2)}) collective-permute-start(bf16[256,2,768]{0,2,1:T(8,128)(2,1)S(1)} %get-tuple-element.1165), channel_id=1, source_target_pairs={{30,0},{31,1}} | collective-permute-start | bytes 2359304 | tf_op jit(solution)/shard_map/while/body/eval_jaxpr/ppermute | solution.py:23
  1545.2 28.9 %collective-permute-start.5 = (bf16[256,2,768]{0,2,1:T(8,128)(2,1)S(1)}, bf16[256,2,768]{0,2,1:T(8,128)(2,1)}, u32[]{:S(2)}, u32[]{:S(2)}) collective-permute-start(bf16[256,2,768]{0,2,1:T(8,128)(2,1)S(1)} %get-tuple-element.1165), channel_id=1, source_target_pairs={{0,2},{2,4},{4,6},{6,8},{8,10},{10,12},{12,14},{14,16},{16,18},{18... | collective-permute-start | bytes 2359304 | tf_op jit(solution)/shard_map/while/body/eval_jaxpr/ppermute | solution.py:23
  1606.9 29.3 %collective-permute-start.4 = (bf16[256,2,768]{0,2,1:T(8,128)(2,1)S(1)}, bf16[256,2,768]{0,2,1:T(8,128)(2,1)S(1)}, u32[]{:S(2)}, u32[]{:S(2)}) collective-permute-start(bf16[256,2,768]{0,2,1:T(8,128)(2,1)S(1)} %get-tuple-element.1165), channel_id=1, source_target_pairs={{30,0},{31,1}} | collective-permute-start | bytes 2359304 | tf_op jit(solution)/shard_map/while/body/eval_jaxpr/ppermute | solution.py:23
  1608.2 28.0 %collective-permute-start.5 = (bf16[256,2,768]{0,2,1:T(8,128)(2,1)S(1)}, bf16[256,2,768]{0,2,1:T(8,128)(2,1)}, u32[]{:S(2)}, u32[]{:S(2)}) collective-permute-start(bf16[256,2,768]{0,2,1:T(8,128)(2,1)S(1)} %get-tuple-element.1165), channel_id=1, source_target_pairs={{0,2},{2,4},{4,6},{6,8},{8,10},{10,12},{12,14},{14,16},{16,18},{18... | collective-permute-start | bytes 2359304 | tf_op jit(solution)/shard_map/while/body/eval_jaxpr/ppermute | solution.py:23
  1669.9 28.6 %collective-permute-start.4 = (bf16[256,2,768]{0,2,1:T(8,128)(2,1)S(1)}, bf16[256,2,768]{0,2,1:T(8,128)(2,1)S(1)}, u32[]{:S(2)}, u32[]{:S(2)}) collective-permute-start(bf16[256,2,768]{0,2,1:T(8,128)(2,1)S(1)} %get-tuple-element.1165), channel_id=1, source_target_pairs={{30,0},{31,1}} | collective-permute-start | bytes 2359304 | tf_op jit(solution)/shard_map/while/body/eval_jaxpr/ppermute | solution.py:23
  1671.1 27.3 collective-permute-start.5
  1732.8 28.6 %collective-permute-start.4 = (bf16[256,2,768]{0,2,1:T(8,128)(2,1)S(1)}, bf16[256,2,768]{0,2,1:T(8,128)(2,1)S(1)}, u32[]{:S(2)}, u32[]{:S(2)}) collective-permute-start(bf16[256,2,768]{0,2,1:T(8,128)(2,1)S(1)} %get-tuple-element.1165), channel_id=1, source_target_pairs={{30,0},{31,1}} | collective-permute-start | bytes 2359304 | tf_op jit(solution)/shard_map/while/body/eval_jaxpr/ppermute | solution.py:23
  1734.1 27.3 collective-permute-start.5
  1795.8 28.6 %collective-permute-start.4 = (bf16[256,2,768]{0,2,1:T(8,128)(2,1)S(1)}, bf16[256,2,768]{0,2,1:T(8,128)(2,1)S(1)}, u32[]{:S(2)}, u32[]{:S(2)}) collective-permute-start(bf16[256,2,768]{0,2,1:T(8,128)(2,1)S(1)} %get-tuple-element.1165), channel_id=1, source_target_pairs={{30,0},{31,1}} | collective-permute-start | bytes 2359304 | tf_op jit(solution)/shard_map/while/body/eval_jaxpr/ppermute | solution.py:23
  1797.1 27.3 collective-permute-start.5
  1858.7 28.6 %collective-permute-start.4 = (bf16[256,2,768]{0,2,1:T(8,128)(2,1)S(1)}, bf16[256,2,768]{0,2,1:T(8,128)(2,1)S(1)}, u32[]{:S(2)}, u32[]{:S(2)}) collective-permute-start(bf16[256,2,768]{0,2,1:T(8,128)(2,1)S(1)} %get-tuple-element.1165), channel_id=1, source_target_pairs={{30,0},{31,1}} | collective-permute-start | bytes 2359304 | tf_op jit(solution)/shard_map/while/body/eval_jaxpr/ppermute | solution.py:23
  1860.0 27.3 collective-permute-start.5
  1921.7 28.6 %collective-permute-start.4 = (bf16[256,2,768]{0,2,1:T(8,128)(2,1)S(1)}, bf16[256,2,768]{0,2,1:T(8,128)(2,1)S(1)}, u32[]{:S(2)}, u32[]{:S(2)}) collective-permute-start(bf16[256,2,768]{0,2,1:T(8,128)(2,1)S(1)} %get-tuple-element.1165), channel_id=1, source_target_pairs={{30,0},{31,1}} | collective-permute-start | bytes 2359304 | tf_op jit(solution)/shard_map/while/body/eval_jaxpr/ppermute | solution.py:23
  1923.0 27.3 collective-permute-start.5
  1988.4 240.3 %collective-permute-start.8 = (bf16[16,2,384]{2,0,1:T(8,128)(2,1)}, bf16[16,2,384]{2,0,1:T(8,128)(2,1)}, u32[]{:S(2)}, u32[]{:S(2)}) collective-permute-start(bf16[16,2,384]{2,0,1:T(8,128)(2,1)} %copy.1134), channel_id=1, source_target_pairs={{0,2},{2,4},{4,6},{6,8},{8,10},{10,12},{12,14},{14,16},{16,18},{18... | collective-permute-start | bytes 73736 | tf_op jit(solution)/shard_map/ppermute | solution.py:31
  1995.2 239.8 %collective-permute-start.9 = (bf16[16,2,384]{2,0,1:T(8,128)(2,1)}, bf16[16,2,384]{2,0,1:T(8,128)(2,1)}, u32[]{:S(2)}, u32[]{:S(2)}) collective-permute-start(bf16[16,2,384]{2,0,1:T(8,128)(2,1)} %copy.1153), channel_id=1, source_target_pairs={{2,0},{4,2},{6,4},{8,6},{10,8},{12,10},{14,12},{16,14},{18,16},{20... | collective-permute-start | bytes 73736 | tf_op jit(solution)/shard_map/ppermute | solution.py:34
  2334.2 442.1 %all-reduce.19.cloned.1.call-start = ((), (), s32[]{:S(2)}) async-start(), calls=%async_computation.4 | async-start | bytes 28311552 | tf_op jit(solution)/shard_map/psum | solution.py:371
  (414 other events, 6001.5 us)
Sparse Core Ops, SparseCore 0:
  796.6 29.6 all-reduce.10
  865.0 30.3 all-reduce.12
  930.2 30.2 all-reduce.14
  2334.4 32.5 all-reduce.16
  2374.4 401.9 all-reduce.18
where the time goes:
time: 2820 us; the launch traced here: 2800 us
  matrix products  1000 us (35%)
  waiting for transfers between devices  656 us (23%)
  local copies, waits for them, and re-layouts  537 us (19%)
  starting transfers between devices  259 us (9%)
  other arithmetic  194 us (7%)
  blocking collectives  85.6 us (3%)
  loops' own time  48.3 us (2%)
    ppermute x90, waiting for transfers between devices, passed_along(): return lax.ppermute(x, axis, pairs)  348 us
    ppermute x90, starting transfers between devices, passed_along(): return lax.ppermute(x, axis, pairs)  243 us
    psum x1, waiting for transfers between devices, shards(): lax.psum((query_grad, key_grad, value_grad, kernel_grad, out_grad, gain_o...  231 us
    convert_element_type x96, local copies, waits for them, and re-layouts, tap_sum(): padded[tap_index:tap_index + length] * kernel[:, tap_index][:, None]  195 us
    dot_general x16, matrix products, key_side(): jnp.einsum('ihab,aihe->bihe', slope_low, query_part, preferred_element_ty...  181 us
    dot_general x31, matrix products, pair_cosine(): jnp.einsum('aihe,bihe->ihab', query_part, key_part, preferred_element_typ...  163 us
    dot_general x16, matrix products, attend_pack(): jnp.einsum('ihab,bihe->aihe', weights_low, second_half(packed), preferred...  144 us
    dot_general x16, matrix products, key_side(): jnp.einsum('ihab,aihe->bihe', weights_low, grad_part, preferred_element_t...  100 us
  transfers between devices with their start and end apart: 99, of which 34 were waited for; matrix products, arithmetic and copies ran while one was open for 29% of the time, Pallas kernels for 0%

commit v1 on v0

v1 whole, which is shorter than its diff:
```python
import math

import jax
import jax.numpy as jnp
from jax import lax
from jax.experimental import pallas as pl
from jax.experimental.pallas import tpu as pltpu
from jax.sharding import PartitionSpec as P

TAU = 8
CONV_WIDTH = 33
HALF_WIDTH = 16
GROUP = 16
PIECE = 256
ITEMS = 2
REACH = 128

COS_SCALE = 0.98
EPS_UNIT = 1e-06
EPS_NORM = 1e-05
NEAR_POLY = (1.158024787902832, -0.36302468180656433, 0.09245320409536362, -0.011449637822806835)
SLOPE_SCALE = TAU / math.pi
VMEM_BYTES = 60 * 2**20

F32 = jnp.float32
BF16 = jnp.bfloat16


def layer_norm(values, gain, bias):
    row_mean = jnp.mean(values, axis=-1, keepdims=True)
    centered = values - row_mean
    variance = jnp.mean(centered * centered, axis=-1, keepdims=True)
    return centered * lax.rsqrt(variance + EPS_NORM) * gain + bias


def exact_gelu(values):
    return jax.nn.gelu(values, approximate=False)


def contract(left, right, left_dim, right_dim):
    return lax.dot_general(
        left, right, (((left_dim,), (right_dim,)), ((), ())), preferred_element_type=F32
    )


def pair_terms(dots, same=None):
    upper = 1.0 / COS_SCALE + dots
    lower = 1.0 / COS_SCALE - dots
    upper_inv = lax.rsqrt(upper)
    lower_inv = lax.rsqrt(lower)
    wide = 1.0 / 0.7 + lower * lower_inv
    wide_inv = lax.rsqrt(wide)
    root = wide * wide_inv
    ratio = NEAR_POLY[3] * root + NEAR_POLY[2]
    ratio = ratio * root + NEAR_POLY[1]
    ratio = ratio * root + NEAR_POLY[0]
    near = ratio * ((upper * upper_inv) * wide_inv)
    if same is not None:
        near = jnp.where(same, near, 0.0)
    near_2 = near * near
    near_4 = near_2 * near_2
    weights = (near_4 * near_4).astype(BF16)
    slopes = ((near_4 * near_2) * (near * (upper_inv * lower_inv))).astype(BF16)
    return weights, slopes


def pad_lanes(dst, src, length):
    dst[:, pl.ds(0, REACH)] = jnp.zeros((dst.shape[0], REACH), dst.dtype)
    dst[:, pl.ds(REACH, length)] = src
    dst[:, pl.ds(REACH + length, REACH)] = jnp.zeros((dst.shape[0], REACH), dst.dtype)


def rows_of(dst, src, length):
    for start in range(0, length, PIECE):
        dst[pl.ds(start, PIECE), :] = src[:, pl.ds(start, PIECE)].T


def long_forward(query, key, value, band):
    head_dim, length = query.shape
    blocks = length // PIECE
    step = 512

    def body(q_ref, k_ref, v_ref, band_ref, o_ref, w_ref, s_ref, key_rows, value_pad):
        block = pl.program_id(0)

        @pl.when(block == 0)
        def _():
            rows_of(key_rows, k_ref, length)
            pad_lanes(value_pad, v_ref[...], length)

        q = q_ref[...]
        start = pl.multiple_of(block * PIECE, PIECE)
        total = contract(value_pad[:, pl.ds(start, PIECE + 2 * REACH)], band_ref[...], 1, 1)
        for at in range(0, length, step):
            dots = contract(key_rows[pl.ds(at, step), :], q, 1, 0)
            weights, slopes = pair_terms(dots)
            w_ref[pl.ds(at, step), :] = weights
            s_ref[pl.ds(at, step), :] = slopes
            total = total + contract(v_ref[:, pl.ds(at, step)], weights, 1, 0)
        o_ref[...] = total.astype(BF16)

    whole = pl.BlockSpec((head_dim, length), lambda i: (0, 0))
    large = pl.BlockSpec((None, length, PIECE), lambda i: (i, 0, 0))
    large_shape = jax.ShapeDtypeStruct((blocks, length, PIECE), BF16)
    return pl.pallas_call(
        body,
        grid=(blocks,),
        in_specs=[
            pl.BlockSpec((head_dim, PIECE), lambda i: (0, i)),
            whole,
            whole,
            pl.BlockSpec((PIECE, PIECE + 2 * REACH), lambda i: (0, 0)),
        ],
        out_specs=[pl.BlockSpec((None, head_dim, PIECE), lambda i: (i, 0, 0)), large, large],
        out_shape=[jax.ShapeDtypeStruct((blocks, head_dim, PIECE), BF16), large_shape, large_shape],
        scratch_shapes=[
            pltpu.VMEM((length, head_dim), BF16),
            pltpu.VMEM((head_dim, length + 2 * REACH), BF16),
        ],
        compiler_params=pltpu.CompilerParams(vmem_limit_bytes=VMEM_BYTES),
        cost_estimate=pl.CostEstimate(
            flops=length * length * 300, bytes_accessed=length * length * 4, transcendentals=0
        ),
    )(query, key, value, band)


def long_backward(query, key, value, grad, band, weights, slopes):
    head_dim, length = query.shape
    blocks = length // PIECE
    step = 1024

    def body(
        q_ref, k_ref, v_ref, g_ref, band_ref, w_ref, s_ref,
        dq_ref, dk_ref, dv_ref, taps_ref, value_rows, value_pad, grad_pad, key_sum, value_sum,
    ):
        block = pl.program_id(0)

        @pl.when(block == 0)
        def _():
            rows_of(value_rows, v_ref, length)
            pad_lanes(value_pad, v_ref[...], length)
            pad_lanes(grad_pad, g_ref[...], length)
            key_sum[...] = jnp.zeros_like(key_sum)
            value_sum[...] = jnp.zeros_like(value_sum)
            taps_ref[...] = jnp.zeros_like(taps_ref)

        start = pl.multiple_of(block * PIECE, PIECE)
        q = q_ref[...]
        g = g_ref[:, pl.ds(start, PIECE)]
        near_values = value_pad[:, pl.ds(start, PIECE + 2 * REACH)]
        near_grads = grad_pad[:, pl.ds(start, PIECE + 2 * REACH)]
        taps_ref[...] += contract(g.T, near_values, 1, 0)
        value_sum[:, pl.ds(start, PIECE)] += contract(near_grads, band_ref[...], 1, 1)
        total = jnp.zeros((head_dim, PIECE), F32)
        for at in range(0, length, step):
            grad_weights = contract(value_rows[pl.ds(at, step), :], g, 1, 0)
            terms = grad_weights.astype(BF16) * s_ref[pl.ds(at, step), :]
            total = total + contract(k_ref[:, pl.ds(at, step)], terms, 1, 0)
            key_sum[:, pl.ds(at, step)] += contract(q, terms, 1, 1)
            value_sum[:, pl.ds(at, step)] += contract(g, w_ref[pl.ds(at, step), :], 1, 1)
        dq_ref[...] = (total * SLOPE_SCALE).astype(BF16)

        @pl.when(block == blocks - 1)
        def _():
            for index in range(blocks):
                piece = pl.ds(index * PIECE, PIECE)
                dk_ref[index] = (key_sum[:, piece] * SLOPE_SCALE).astype(BF16)
                dv_ref[index] = value_sum[:, piece].astype(BF16)

    whole = pl.BlockSpec((head_dim, length), lambda i: (0, 0))
    large = pl.BlockSpec((None, length, PIECE), lambda i: (i, 0, 0))
    pieces = pl.BlockSpec((blocks, head_dim, PIECE), lambda i: (0, 0, 0))
    pieces_shape = jax.ShapeDtypeStruct((blocks, head_dim, PIECE), BF16)
    wide = PIECE + 2 * REACH
    return pl.pallas_call(
        body,
        grid=(blocks,),
        in_specs=[
            pl.BlockSpec((head_dim, PIECE), lambda i: (0, i)),
            whole,
            whole,
            whole,
            pl.BlockSpec((PIECE, wide), lambda i: (0, 0)),
            large,
            large,
        ],
        out_specs=[
            pl.BlockSpec((None, head_dim, PIECE), lambda i: (i, 0, 0)),
            pieces,
            pieces,
            pl.BlockSpec((PIECE, wide), lambda i: (0, 0)),
        ],
        out_shape=[pieces_shape] * 3 + [jax.ShapeDtypeStruct((PIECE, wide), F32)],
        scratch_shapes=[
            pltpu.VMEM((length, head_dim), BF16),
            pltpu.VMEM((head_dim, length + 2 * REACH), BF16),
            pltpu.VMEM((head_dim, length + 2 * REACH), BF16),
            pltpu.VMEM((head_dim, length), F32),
            pltpu.VMEM((head_dim, length), F32),
        ],
        compiler_params=pltpu.CompilerParams(vmem_limit_bytes=VMEM_BYTES),
        cost_estimate=pl.CostEstimate(
            flops=length * length * 300, bytes_accessed=length * length * 4, transcendentals=0
        ),
    )(query, key, value, grad, band, weights, slopes)


def short_forward(reach, ids_row, ids_col, query, key, value, band):
    heads, head_dim, length = query.shape
    blocks = length // PIECE
    wide = PIECE + 2 * REACH

    def body(
        reach_ref, row_ref, col_ref, q_ref, k_ref, v_ref, band_ref,
        o_ref, w_ref, s_ref, key_rows, value_pad, total,
    ):
        block = pl.program_id(0)

        @pl.when(block == 0)
        def _():
            for h in range(heads):
                rows_of(key_rows.at[h], k_ref.at[h], length)
                pad_lanes(value_pad.at[h], v_ref[h], length)

        start = pl.multiple_of(block * PIECE, PIECE)
        near = (col_ref[pl.ds(start, PIECE), :] == row_ref[:, pl.ds(start, wide)]).astype(F32)
        for h in range(heads):
            masked = (band_ref[h] * near).astype(BF16)
            total[h] = contract(value_pad[h, :, pl.ds(start, wide)], masked, 1, 1)

        own_ids = row_ref[:, pl.ds(start + REACH, PIECE)]

        def turn(step, carry):
            at = pl.multiple_of(step * PIECE, PIECE)
            same = col_ref[pl.ds(at, PIECE), :] == own_ids
            for h in range(heads):
                dots = contract(key_rows[h, pl.ds(at, PIECE), :], q_ref[h], 1, 0)
                weights, slopes = pair_terms(dots, same)
                w_ref[h, pl.ds(at, PIECE), :] = weights
                s_ref[h, pl.ds(at, PIECE), :] = slopes
                total[h] += contract(v_ref[h, :, pl.ds(at, PIECE)], weights, 1, 0)
            return carry

        lax.fori_loop(reach_ref[0, block], reach_ref[1, block], turn, 0)
        o_ref[...] = total[...].astype(BF16)

    whole = pl.BlockSpec((heads, head_dim, length), lambda i: (0, 0, 0))
    block_spec = pl.BlockSpec((heads, head_dim, PIECE), lambda i: (0, 0, i))
    large = pl.BlockSpec((None, heads, length, PIECE), lambda i: (i, 0, 0, 0))
    large_shape = jax.ShapeDtypeStruct((blocks, heads, length, PIECE), BF16)
    return pl.pallas_call(
        body,
        grid=(blocks,),
        in_specs=[
            pl.BlockSpec(memory_space=pltpu.SMEM),
            pl.BlockSpec((1, length + 2 * REACH), lambda i: (0, 0)),
            pl.BlockSpec((length, 1), lambda i: (0, 0)),
            block_spec,
            whole,
            whole,
            pl.BlockSpec((heads, PIECE, wide), lambda i: (0, 0, 0)),
        ],
        out_specs=[block_spec, large, large],
        out_shape=[jax.ShapeDtypeStruct((heads, head_dim, length), BF16), large_shape, large_shape],
        scratch_shapes=[
            pltpu.VMEM((heads, length, head_dim), BF16),
            pltpu.VMEM((heads, head_dim, length + 2 * REACH), BF16),
            pltpu.VMEM((heads, head_dim, PIECE), F32),
        ],
        compiler_params=pltpu.CompilerParams(vmem_limit_bytes=VMEM_BYTES),
        cost_estimate=pl.CostEstimate(
            flops=heads * length * length * 200,
            bytes_accessed=heads * length * length * 4,
            transcendentals=0,
        ),
    )(reach, ids_row, ids_col, query, key, value, band)


def short_backward(reach, ids_row, ids_col, query, key, value, grad, band, weights, slopes):
    heads, head_dim, length = query.shape
    blocks = length // PIECE
    wide = PIECE + 2 * REACH

    def body(
        reach_ref, row_ref, col_ref, q_ref, k_ref, v_ref, g_ref, band_ref, w_ref, s_ref,
        dq_ref, dk_ref, dv_ref, taps_ref, value_rows, value_pad, grad_pad,
    ):
        block = pl.program_id(0)

        @pl.when(block == 0)
        def _():
            for h in range(heads):
                rows_of(value_rows.at[h], v_ref.at[h], length)
                pad_lanes(value_pad.at[h], v_ref[h], length)
                pad_lanes(grad_pad.at[h], g_ref[h], length)
            dk_ref[...] = jnp.zeros_like(dk_ref)
            dv_ref[...] = jnp.zeros_like(dv_ref)
            taps_ref[...] = jnp.zeros_like(taps_ref)

        start = pl.multiple_of(block * PIECE, PIECE)
        near = (col_ref[pl.ds(start, PIECE), :] == row_ref[:, pl.ds(start, wide)]).astype(F32)
        for h in range(heads):
            masked = (band_ref[h] * near).astype(BF16)
            own = g_ref[h, :, pl.ds(start, PIECE)]
            taps_ref[h] += contract(own.T, value_pad[h, :, pl.ds(start, wide)], 1, 0) * near
            dv_ref[h, :, pl.ds(start, PIECE)] += contract(
                grad_pad[h, :, pl.ds(start, wide)], masked, 1, 1
            )
        dq_ref[...] = jnp.zeros_like(dq_ref)

        def turn(step, carry):
            at = pl.multiple_of(step * PIECE, PIECE)
            for h in range(heads):
                own = g_ref[h, :, pl.ds(start, PIECE)]
                grad_weights = contract(value_rows[h, pl.ds(at, PIECE), :], own, 1, 0)
                terms = grad_weights.astype(BF16) * s_ref[h, pl.ds(at, PIECE), :]
                dq_ref[h] += contract(k_ref[h, :, pl.ds(at, PIECE)], terms, 1, 0) * SLOPE_SCALE
                dk_ref[h, :, pl.ds(at, PIECE)] += contract(q_ref[h], terms, 1, 1) * SLOPE_SCALE
                dv_ref[h, :, pl.ds(at, PIECE)] += contract(own, w_ref[h, pl.ds(at, PIECE), :], 1, 1)
            return carry

        lax.fori_loop(reach_ref[0, block], reach_ref[1, block], turn, 0)

    whole = pl.BlockSpec((heads, head_dim, length), lambda i: (0, 0, 0))
    block_spec = pl.BlockSpec((heads, head_dim, PIECE), lambda i: (0, 0, i))
    large = pl.BlockSpec((None, heads, length, PIECE), lambda i: (i, 0, 0, 0))
    bands = pl.BlockSpec((heads, PIECE, wide), lambda i: (0, 0, 0))
    whole_shape = jax.ShapeDtypeStruct((heads, head_dim, length), F32)
    return pl.pallas_call(
        body,
        grid=(blocks,),
        in_specs=[
            pl.BlockSpec(memory_space=pltpu.SMEM),
            pl.BlockSpec((1, length + 2 * REACH), lambda i: (0, 0)),
            pl.BlockSpec((length, 1), lambda i: (0, 0)),
            block_spec,
            whole,
            whole,
            whole,
            bands,
            large,
            large,
        ],
        out_specs=[block_spec, whole, whole, bands],
        out_shape=[whole_shape] * 3 + [jax.ShapeDtypeStruct((heads, PIECE, wide), F32)],
        scratch_shapes=[
            pltpu.VMEM((heads, length, head_dim), BF16),
            pltpu.VMEM((heads, head_dim, length + 2 * REACH), BF16),
            pltpu.VMEM((heads, head_dim, length + 2 * REACH), BF16),
        ],
        compiler_params=pltpu.CompilerParams(vmem_limit_bytes=VMEM_BYTES),
        cost_estimate=pl.CostEstimate(
            flops=heads * length * length * 200,
            bytes_accessed=heads * length * length * 4,
            transcendentals=0,
        ),
    )(reach, ids_row, ids_col, query, key, value, grad, band, weights, slopes)


def band_of(taps):
    wide = PIECE + 2 * REACH
    first = REACH - HALF_WIDTH
    line = jnp.pad(taps, ((0, 0), (first, wide + 1 - first - CONV_WIDTH)))
    flat = jnp.tile(line, (1, PIECE))[:, : PIECE * wide]
    return flat.reshape(taps.shape[0], PIECE, wide)


def band_sums(products):
    heads, rows, wide = products.shape
    first = REACH - HALF_WIDTH
    flat = jnp.pad(products.reshape(heads, rows * wide), ((0, 0), (0, rows)))
    return jnp.sum(flat.reshape(heads, rows, wide + 1), axis=1)[:, first : first + CONV_WIDTH]


def across_tp(part):
    own = part.astype(BF16)
    other = lax.ppermute(own, "tp", [(0, 1), (1, 0)])
    return own.astype(F32) + other.astype(F32)


def sum_all(parts, axis):
    peers = lax.axis_size(axis)
    flat = jnp.concatenate([part.reshape(peers, -1, 768).astype(BF16) for part in parts], axis=1)
    pieces = lax.all_to_all(flat, axis, 0, 0)
    own = jnp.sum(pieces.astype(F32), axis=0).astype(BF16)
    gathered = lax.all_gather(own, axis, axis=0).astype(F32)
    sums, at = [], 0
    for part in parts:
        rows = part.size // peers // 768
        sums.append(gathered[:, at : at + rows].reshape(part.shape))
        at += rows
    return sums


def shards(
    tokens,
    short_lengths,
    query_weight,
    key_weight,
    value_weight,
    conv_kernel,
    out_weight,
    gain_one,
    bias_one,
    inner_weight,
    outer_weight,
    gain_two,
    bias_two,
    cotangent,
):
    row_total, width = tokens.shape
    heads_dev = conv_kernel.shape[0]
    head_cols = query_weight.shape[1]
    head_dim = head_cols // heads_dev
    long_rows = ITEMS * PIECE
    short_rows = row_total - long_rows
    units = ITEMS * heads_dev
    place = lax.axis_index("seq") % GROUP
    groups = [
        [first + i for i in range(GROUP)] for first in range(0, lax.axis_size("seq"), GROUP)
    ]

    def by_item(rows):
        long_part = rows[:long_rows].reshape(PIECE, ITEMS, rows.shape[1]).swapaxes(0, 1)
        return jnp.concatenate(
            [long_part.reshape(long_rows, rows.shape[1]), rows[long_rows:]], axis=0
        )

    def by_place(rows):
        long_part = rows[:long_rows].reshape(ITEMS, PIECE, rows.shape[1]).swapaxes(0, 1)
        return jnp.concatenate(
            [long_part.reshape(long_rows, rows.shape[1]), rows[long_rows:]], axis=0
        )

    def to_owner(parts):
        count = parts.shape[0]
        split = parts.reshape(count, heads_dev, head_dim, ITEMS, PIECE)
        split = jnp.transpose(split, (3, 1, 0, 2, 4)).reshape(units, count * head_dim, PIECE)
        split = jnp.pad(split, ((0, GROUP - units), (0, 0), (0, 0)))
        moved = lax.all_to_all(split, "seq", 0, 0, axis_index_groups=groups)
        return jnp.transpose(moved, (1, 0, 2)).reshape(count, head_dim, GROUP * PIECE)

    def from_owner(pieces):
        count = pieces.shape[1]
        moved = lax.all_to_all(pieces, "seq", 0, 0, axis_index_groups=groups)[:units]
        moved = moved.reshape(ITEMS, heads_dev, count, head_dim, PIECE)
        return jnp.transpose(moved, (2, 1, 3, 0, 4)).reshape(count, heads_dev, head_dim, long_rows)

    tokens = by_item(tokens)
    cotangent = by_item(cotangent)

    item_ends = jnp.cumsum(short_lengths[0])
    positions = jnp.arange(short_rows, dtype=jnp.int32)
    item_ids = jnp.sum((positions[:, None] >= item_ends[None, :]).astype(jnp.int32), axis=1)
    ids_row = jnp.pad(item_ids, (REACH, REACH), constant_values=-1)[None, :]
    ids_col = item_ids[:, None]
    item_starts = jnp.concatenate([jnp.zeros((1,), jnp.int32), item_ends[:-1]])
    block_first = jnp.arange(0, short_rows, PIECE, dtype=jnp.int32)
    block_last = block_first + (PIECE - 1)
    inside = (item_starts[None, :] <= block_last[:, None]) & (
        item_ends[None, :] > block_first[:, None]
    )
    lowest = jnp.min(jnp.where(inside, item_starts[None, :], short_rows), axis=1)
    highest = jnp.max(jnp.where(inside, item_ends[None, :], 0), axis=1)
    reach = jnp.stack([lowest // PIECE, (highest + PIECE - 1) // PIECE]).astype(jnp.int32)

    band = band_of(conv_kernel)
    band_back = band_of(conv_kernel[:, ::-1])
    unit_head = place % heads_dev
    long_band = lax.dynamic_index_in_dim(band, unit_head, 0, False).astype(BF16)
    long_band_back = lax.dynamic_index_in_dim(band_back, unit_head, 0, False).astype(BF16)

    weight_all = jnp.concatenate([query_weight, key_weight, value_weight], axis=1)
    projected = contract(weight_all, tokens, 0, 1).reshape(3, heads_dev, head_dim, row_total)
    raw = projected[:2]
    inverse = lax.rsqrt(jnp.sum(raw * raw, axis=2, keepdims=True) + EPS_UNIT)
    unit = raw * inverse
    packed = jnp.concatenate([unit.astype(BF16), projected[2:].astype(BF16)], axis=0)
    long_pack = to_owner(packed[..., :long_rows])
    short_pack = packed[..., long_rows:]

    short_att, short_w, short_s = short_forward(
        reach, ids_row, ids_col, short_pack[0], short_pack[1], short_pack[2], band
    )
    long_att, long_w, long_s = long_forward(long_pack[0], long_pack[1], long_pack[2], long_band)
    long_home = from_owner(long_att[:, None])[0]
    mixed = jnp.concatenate([long_home, short_att], axis=2).reshape(head_cols, row_total)

    hidden = tokens.astype(F32) + across_tp(contract(mixed, out_weight, 0, 0))
    normed, norm_one_back = jax.vjp(layer_norm, hidden, gain_one, bias_one)
    normed_low = normed.astype(BF16)
    pre_act = jnp.dot(normed_low, inner_weight, preferred_element_type=F32)
    act_rows, gelu_back = jax.vjp(exact_gelu, pre_act)
    act_low = act_rows.astype(BF16)
    ffn_out = across_tp(jnp.dot(act_low, outer_weight, preferred_element_type=F32))
    output, norm_two_back = jax.vjp(layer_norm, normed + ffn_out, gain_two, bias_two)
    grad_sum, gain_two_grad, bias_two_grad = norm_two_back(cotangent.astype(F32))
    grad_ffn_low = grad_sum.astype(BF16)
    outer_grad = contract(act_low, grad_ffn_low, 0, 0)
    grad_pre_low = gelu_back(contract(grad_ffn_low, outer_weight, 1, 1))[0].astype(BF16)
    inner_grad = contract(normed_low, grad_pre_low, 0, 0)
    grad_normed = grad_sum + across_tp(contract(grad_pre_low, inner_weight, 1, 1))
    grad_hidden, gain_one_grad, bias_one_grad = norm_one_back(grad_normed)
    grad_proj_low = grad_hidden.astype(BF16)
    grad_att = contract(out_weight, grad_proj_low, 1, 1).astype(BF16)
    grad_att = grad_att.reshape(heads_dev, head_dim, row_total)
    out_grad = contract(mixed, grad_proj_low, 1, 0)

    long_grad = to_owner(grad_att[None, ..., :long_rows])[0]
    short_dq, short_dk, short_dv, short_taps = short_backward(
        reach,
        ids_row,
        ids_col,
        short_pack[0],
        short_pack[1],
        short_pack[2],
        grad_att[..., long_rows:],
        band_back,
        short_w,
        short_s,
    )
    long_dq, long_dk, long_dv, long_taps = long_backward(
        long_pack[0], long_pack[1], long_pack[2], long_grad, long_band_back, long_w, long_s
    )
    owner = (jnp.arange(heads_dev) == unit_head) & (place < units)
    kernel_grad = band_sums(short_taps) + jnp.where(
        owner[:, None], band_sums(long_taps[None]), 0.0
    )
    long_back = from_owner(jnp.stack([long_dq, long_dk, long_dv], axis=1)).astype(F32)
    grads = jnp.concatenate(
        [long_back, jnp.stack([short_dq, short_dk, short_dv], axis=0)], axis=3
    )
    unit_grads = grads[:2]
    along = jnp.sum(unit * unit_grads, axis=2, keepdims=True)
    raw_grads = (unit_grads - unit * along) * inverse
    grads_low = jnp.concatenate([raw_grads, grads[2:]], axis=0).astype(BF16)
    grads_low = grads_low.reshape(3 * head_cols, row_total)
    weight_grads = contract(tokens, grads_low, 0, 1)
    token_grad = grad_hidden + across_tp(contract(grads_low, weight_all, 0, 1))

    inner_sum, outer_sum, out_sum = sum_all([inner_grad, outer_grad, out_grad], "seq")
    (qkv_sum,) = sum_all([weight_grads], "seq")
    small = lax.psum(
        (kernel_grad, gain_one_grad, bias_one_grad, gain_two_grad, bias_two_grad), "seq"
    )
    return (
        by_place(output.astype(BF16)),
        by_place(token_grad),
        qkv_sum[:, :head_cols],
        qkv_sum[:, head_cols : 2 * head_cols],
        qkv_sum[:, 2 * head_cols :],
        small[0],
        out_sum,
        small[1],
        small[2],
        inner_sum,
        outer_sum,
        small[3],
        small[4],
    )


def solution(mesh):
    rows = P("seq", None)
    columns = P(None, "tp")
    split_rows = P("tp", None)
    return jax.shard_map(
        shards,
        mesh=mesh,
        in_specs=(
            rows, rows, columns, columns, columns, split_rows, split_rows,
            P(), P(), columns, split_rows, P(), P(), rows,
        ),
        out_specs=(
            rows, rows, columns, columns, columns, split_rows, split_rows,
            P(), P(), columns, split_rows, P(), P(),
        ),
        check_vma=False,
    )
```

time: 2820 us -> 785 us (0.28)
  matrix products: 1000 us -> 86.2 us
  waiting for transfers between devices: 656 us -> 130 us
  local copies, waits for them, and re-layouts: 537 us -> 141 us
  starting transfers between devices: 259 us -> 36.5 us
  Pallas kernels: 0 us -> 176 us
  other arithmetic: 194 us -> 56.2 us
  blocking collectives: 85.6 us -> 136 us
  loops' own time: 48.3 us -> 0 us
    dot_general x126 -> x12, matrix products: 1000 us -> 86.2 us  [the longest x10 56 us: contract(): lax.dot_general(left, right, (((left_dim,), (right_dim,)), ((), ())), pre...]
    ppermute x94 -> x4, waiting for transfers between devices: 348 us -> 10 us  [across_tp(): other = lax.ppermute(own, 'tp', [(0, 1), (1, 0)])]
    psum x5 -> x0, waiting for transfers between devices: 308 us -> none  [the longest x1 231 us: shards(): lax.psum((query_grad, key_grad, value_grad, kernel_grad, out_grad, gain_o...]
    ppermute x94 -> x4, starting transfers between devices: 258 us -> 0.41 us  [across_tp(): other = lax.ppermute(own, 'tp', [(0, 1), (1, 0)])]
    convert_element_type x96 -> x5, local copies, waits for them, and re-layouts: 195 us -> 14 us  [the longest x2 5.96 us: sum_all(): part.reshape(peers, -1, 768).astype(BF16)]
    pallas_call x0 -> x4, Pallas kernels: none -> 176 us  [the longest x1 72 us: long_forward(): pl.pallas_call(body, grid=(blocks,), in_specs=[pl.BlockSpec((head_dim, PI...]
    all_to_all x0 -> x5, waiting for transfers between devices: none -> 120 us  [the longest x2 114 us: sum_all(): pieces = lax.all_to_all(flat, axis, 0, 0)]
    dynamic_update_slice x8 -> x0, local copies, waits for them, and re-layouts: 67.2 us -> none  [shards(): lax.map(attend_short, (query_blocks, id_blocks))]
  transfers between devices with their start and end apart: 99 -> 11, of which waited for: 34 -> 6; matrix products, arithmetic and copies ran while one was open for 29% -> 17% of each run, Pallas kernels for 0% -> 7%
where the time goes in v1:
time: 785 us; the launch traced here: 778 us
  Pallas kernels  176 us (22%)
  local copies, waits for them, and re-layouts  141 us (18%)
  blocking collectives  136 us (17%)
  waiting for transfers between devices  130 us (17%)
  matrix products  86.2 us (11%)
  other arithmetic  56.2 us (7%)
  starting transfers between devices  36.5 us (5%)
  between operations  15.5 us (2%)
    all_to_all x2, waiting for transfers between devices, sum_all(): pieces = lax.all_to_all(flat, axis, 0, 0)  114 us
    psum x1, blocking collectives, shards(): lax.psum((kernel_grad, gain_one_grad, bias_one_grad, gain_two_grad, bias_...  105 us
    pallas_call x1, Pallas kernels, long_forward(): pl.pallas_call(body, grid=(blocks,), in_specs=[pl.BlockSpec((head_dim, PI...  72 us
    dot_general x10, matrix products, contract(): lax.dot_general(left, right, (((left_dim,), (right_dim,)), ((), ())), pre...  56 us
    pallas_call x1, Pallas kernels, long_backward(): pl.pallas_call(body, grid=(blocks,), in_specs=[pl.BlockSpec((head_dim, PI...  49.2 us
    all_to_all x1, blocking collectives, to_owner(): moved = lax.all_to_all(split, 'seq', 0, 0, axis_index_groups=groups)  31.2 us
    pallas_call x1, Pallas kernels, short_forward(): pl.pallas_call(body, grid=(blocks,), in_specs=[pl.BlockSpec(memory_space=...  28.7 us
    pallas_call x1, Pallas kernels, short_backward(): pl.pallas_call(body, grid=(blocks,), in_specs=[pl.BlockSpec(memory_space=...  25.9 us
  transfers between devices with their start and end apart: 11, of which 6 were waited for; matrix products, arithmetic and copies ran while one was open for 17% of the time, Pallas kernels for 7%

profile of v1, /device:TPU:0, one launch (start us, length us, event | category | flops | bytes accessed | tf_op | source)
XLA Modules:
  0.0 778.3 jit_solution(15864074316391206665)
XLA Ops:
  16.3 3.0 fusion.29
  24.5 3.7 reshape.351
  31.1 8.6 %all-to-all-start = ((bf16[16,192,256]{2,1,0:T(8,128)(2,1)}), bf16[16,192,256]{2,1,0:T(8,128)(2,1)}, u32[]{:S(2)}, u32[]{:S(2)}) async-start(bf16[16,192,256]{2,1,0:T(8,128)(2,1)} %pad.27), calls=%async_computation | async-start | bytes 3145728 | tf_op jit(solution)/shard_map/all_to_all | solution.py:440
  43.0 2.9 tile.8
  45.9 7.1 tile.9
  55.2 3.5 copy.98
  60.9 7.1 tile.21
  70.2 3.4 copy.97
  80.3 72.0 %shard_map.237 = (bf16[16,64,256]{2,1,0:T(8,128)(2,1)}, bf16[16,4096,256]{2,1,0:T(8,128)(2,1)}, bf16[16,4096,256]{2,1,0:T(8,128)(2,1)}) custom-call(bf16[64,4096]{1,0:T(8,128)(2,1)} %bitcast.177, bf16[64,4096]{1,0:T(8,128)(2,1)} %bitcast.175, bf16[64,4096]{1,0:T(8,128)(2,1)} %bitcast.173, bf16[256,512]{1,0:T(8,128)(2,1)} %get-tuple-element.82.band_ref), custom_call_target="tpu_custom_call" | custom-call | flops 5033164800 | bytes 67108864 | tf_op jit(solution)/shard_map/pallas_call | solution.py:105
  152.3 7.5 all-to-all-start.1
  164.2 28.7 %shard_map.238 = (bf16[6,64,1024]{2,1,0:T(8,128)(2,1)}, bf16[4,6,1024,256]{3,2,1,0:T(8,128)(2,1)}, bf16[4,6,1024,256]{3,2,1,0:T(8,128)(2,1)}) custom-call(s32[2,4]{1,0:T(2,128)} %pad_add_fusion.reach_ref, s32[1,1280]{1,0:T(1,128)} %broadcast_in_dim.81.row_ref, s32[1024,1]{1,0:T(8,128)} %copy.72.col_ref, bf16[6,64,1024]{2,1,0:T(8,128)(2,1)} %get-tuple-element.72.q_ref, ...), custom_call_target="tpu_custom_call" | custom-call | flops 1258291200 | bytes 25165824 | tf_op jit(solution)/shard_map/pallas_call | solution.py:251
  197.9 4.5 collective-permute-done
  204.2 25.2 %multiply_convert_fusion = (bf16[1536,1536]{1,0:T(8,128)(2,1)S(1)}, f32[1536,1536]{1,0:T(8,128)}, f32[1536,1536]{1,0:T(8,128)}) fusion(bf16[768,1536]{1,0:T(8,128)(2,1)S(1)} %copy-done, f32[1536,768]{1,0:T(8,128)S(1)} %get-tuple-element.64, f32[768]{0:T(1024)S(1)} %copy-done.37, f32[768]{0:T(1024)S(1)} %copy-done.24, f32[1536]{0:T(1024)S(1)} %fusion.32, ...), kind=kOutput, calls=%fused_computation.4 | convolution fusion | flops 3783131136 | bytes 30689280 | tf_op jit(solution)/shard_map/dot_general | solution.py:492
  229.4 5.0 convolution_convert_fusion.5
  239.3 5.0 fusion.43
  245.8 3.8 fusion.10
  249.6 4.3 fusion.42
  254.0 13.4 %add_convert_fusion = bf16[1536,1536]{1,0:T(8,128)(2,1)} fusion(f32[1536,1536]{1,0:T(8,128)} %get-tuple-element.62, bf16[1536,768]{1,0:T(8,128)(2,1)S(1)} %copy-done.40, f32[1536,1536]{1,0:T(8,128)} %get-tuple-element.78, f32[1536,768]{1,0:T(8,128)S(1)} %get-tuple-element.58, f32[1536]{0:T(1024)S(1)} %negate_multiply_fusion.2), kind=kOutput, calls=%fused_computation.3 | convolution fusion | flops 3659268096 | bytes 30676992 | tf_op jit(solution)/shard_map/dot_general | solution.py:41
  267.4 6.2 convolution_convert_fusion.4
  273.8 4.4 collective-permute-done.2
  278.2 3.7 multiply_reduce_fusion
  288.3 31.2 %all_to_all.30 = bf16[16,64,256]{2,1,0:T(8,128)(2,1)S(1)} all-to-all(bf16[16,64,256]{2,1,0:T(8,128)(2,1)S(1)} %pad.30), channel_id=1, replica_groups={{0,2,4,6,8,10,12,14,16,18,20,22,24,26,28,30},{1,3,5,7,9,11,13,15,17,19,..., dimensions={0} | all-to-all | bytes 1048576 | tf_op jit(solution)/shard_map/all_to_all | solution.py:440
  320.3 49.2 %shard_map.239 = (bf16[16,64,256]{2,1,0:T(8,128)(2,1)}, bf16[16,64,256]{2,1,0:T(8,128)(2,1)}, bf16[16,64,256]{2,1,0:T(8,128)(2,1)}, f32[256,512]{1,0:T(8,128)}) custom-call(bf16[64,4096]{1,0:T(8,128)(2,1)} %bitcast.178, bf16[64,4096]{1,0:T(8,128)(2,1)} %bitcast.176, bf16[64,4096]{1,0:T(8,128)(2,1)} %bitcast.174, bf16[64,4096]{1,0:T(8,128)(2,1)} %bitcast.179, ...), custom_call_target="tpu_custom_call" | custom-call | flops 5033164800 | bytes 67108864 | tf_op jit(solution)/shard_map/pallas_call | solution.py:175
  372.4 3.9 all-to-all-start.3
  377.3 25.9 %shard_map.240 = (f32[6,64,1024]{2,1,0:T(8,128)}, f32[6,64,1024]{2,1,0:T(8,128)}, f32[6,64,1024]{2,1,0:T(8,128)}, f32[6,256,512]{2,1,0:T(8,128)}) custom-call(s32[2,4]{1,0:T(2,128)} %pad_add_fusion.reach_ref, s32[1,1280]{1,0:T(1,128)} %broadcast_in_dim.81.row_ref, s32[1024,1]{1,0:T(8,128)} %copy.72.col_ref, bf16[6,64,1024]{2,1,0:T(8,128)(2,1)} %get-tuple-element.72.q_ref, ...), custom_call_target="tpu_custom_call" | custom-call | flops 1258291200 | bytes 25165824 | tf_op jit(solution)/shard_map/pallas_call | solution.py:329
  403.2 6.8 all-to-all-done.3
  412.7 3.3 reshape.373
  423.2 3.3 convolution_convert_fusion.2
  428.9 7.5 all-to-all-start.4
  436.7 9.6 %convolution_convert_fusion.1 = bf16[768,1536]{1,0:T(8,128)(2,1)} fusion(bf16[1536,1536]{1,0:T(8,128)(2,1)} %add_convert_fusion, f32[1536,768]{1,0:T(8,128)} %copy-done.2, f32[768]{0:T(1024)S(1)} %copy-done.38, f32[768]{0:T(1024)S(1)} %copy-done.25, f32[1536]{0:T(1024)S(1)} %fusion.32, f32[1536]{0:T(1024)S(1)} %broadcast_multiply_fusion.1), kind=kOutput, calls=%fused_computation.52 | convolution fusion | flops 3630956544 | bytes 11814912 | tf_op jit(solution)/shard_map/dot_general | solution.py:41
  446.3 3.6 convert_element_type.188
  449.9 8.0 %convolution_convert_fusion = bf16[1536,768]{1,0:T(8,128)(2,1)S(1)} fusion(bf16[1536,1536]{1,0:T(8,128)(2,1)} %copy-done.45, f32[1536,768]{1,0:T(8,128)} %copy-done.5, f32[1536]{0:T(1024)S(1)} %copy-done.27), kind=kOutput, calls=%fused_computation.51 | convolution fusion | flops 3627417600 | bytes 11802624 | tf_op jit(solution)/shard_map/dot_general | solution.py:41
  462.1 11.3 %all-to-all-done.4 = bf16[16,72,768]{2,1,0:T(8,128)(2,1)} async-done(((bf16[16,72,768]{2,1,0:T(8,128)(2,1)}), bf16[16,72,768]{2,1,0:T(8,128)(2,1)}, u32[]{:S(2)}, u32[]{:S(2)}) %all-to-all-start.4) | async-done | bytes 1769504 | tf_op jit(solution)/shard_map/all_to_all | solution.py:384
  473.4 8.2 %all-to-all-start.5 = ((bf16[16,216,768]{2,1,0:T(8,128)(2,1)}), bf16[16,216,768]{2,1,0:T(8,128)(2,1)}, u32[]{:S(2)}, u32[]{:S(2)}) async-start(bf16[16,216,768]{2,1,0:T(8,128)(2,1)} %pad_maximum_fusion), calls=%async_computation.5 | async-start | bytes 10616832 | tf_op jit(solution)/shard_map/all_to_all | solution.py:384
  484.3 102.3 %all-to-all-done.5 = bf16[16,216,768]{2,1,0:T(8,128)(2,1)} async-done(((bf16[16,216,768]{2,1,0:T(8,128)(2,1)}), bf16[16,216,768]{2,1,0:T(8,128)(2,1)}, u32[]{:S(2)}, u32[]{:S(2)}) %all-to-all-start.5) | async-done | bytes 5308448 | tf_op jit(solution)/shard_map/all_to_all | solution.py:384
  586.6 4.1 reduce_sum.226
  590.8 7.4 convolution_convert_fusion.3
  600.6 3.0 pad_maximum_fusion.4
  603.6 3.8 copy.88
  609.8 7.7 reshape.368
  620.4 5.4 pad_reduce_fusion
  626.6 104.9 %all-reduce.7 = (f32[6,33]{1,0:T(8,128)}, f32[768]{0:T(1024)}, f32[768]{0:T(1024)}, f32[768]{0:T(1024)}, f32[768]{0:T(1024)}) all-reduce(f32[6,33]{1,0:T(8,128)S(1)} %slice_add_fusion, f32[768]{0:T(1024)S(1)} %copy-done.33, f32[768]{0:T(1024)S(1)} %copy-done.34, f32[768]{0:T(1024)S(1)} %copy-done.31, ...), channel_id=1, replica_groups=mesh['seq'=16,'tp'=2] {'seq'}, use_global_device_ids=true, to_apply=%region_17.18 | all-reduce | flops 3270 | bytes 26160 | tf_op jit(solution)/shard_map/psum | solution.py:543
  731.6 4.6 add_add_fusion.2
  742.8 4.4 pad_maximum_fusion.1
  747.2 4.2 reshape.375
  751.4 3.9 fusion.47
  757.4 7.3 fusion.46
  764.7 6.2 reshape.371
  (222 shorter events, 98.8 us)
Async XLA Ops:
  7.2 197.0 %copy-start = (bf16[768,1536]{1,0:T(8,128)(2,1)S(1)}, bf16[768,1536]{1,0:T(8,128)(2,1)}, u32[]{:S(2)}) copy-start(bf16[768,1536]{1,0:T(8,128)(2,1)} %param.23) | copy-start | bytes 7077892
  11.2 5.1 copy-start.9
  12.6 6.8 copy-start.15
  28.2 11.5 %copy-start.44 = (s32[1,3]{1,0:T(1,128)S(1)}, s32[1,3]{1,0:T(1,128)}, u32[]{:S(2)}) copy-start(s32[1,3]{1,0:T(1,128)} %param.15) | copy-start | bytes 40
  28.2 11.7 %copy-start.35 = (f32[6,33]{1,0:T(8,128)S(1)}, f32[6,33]{1,0:T(8,128)}, u32[]{:S(2)}) copy-start(f32[6,33]{1,0:T(8,128)} %param.19) | copy-start | bytes 2380
  31.1 45.1 %all-to-all-start = ((bf16[16,192,256]{2,1,0:T(8,128)(2,1)}), bf16[16,192,256]{2,1,0:T(8,128)(2,1)}, u32[]{:S(2)}, u32[]{:S(2)}) async-start(bf16[16,192,256]{2,1,0:T(8,128)(2,1)} %pad.27), calls=%async_computation | async-start | bytes 3145728 | tf_op jit(solution)/shard_map/all_to_all | solution.py:440
  53.0 5.7 copy-start.23
  152.3 40.7 %all-to-all-start.1 = ((bf16[16,1,64,256]{3,2,1,0:T(8,128)(2,1)}), bf16[16,1,64,256]{3,2,1,0:T(8,128)(2,1)}, u32[]{:S(2)}, u32[]{:S(2)}) async-start(bf16[16,1,64,256]{3,2,1,0:T(8,128)(2,1)} %bitcast.191), calls=%async_computation.1 | async-start | bytes 1048576 | tf_op jit(solution)/shard_map/all_to_all | solution.py:445
  164.2 30.9 %copy-start.42 = (bf16[384,768]{1,0:T(8,128)(2,1)S(1)}, bf16[384,768]{1,0:T(8,128)(2,1)}, u32[]{:S(2)}) copy-start(bf16[384,768]{1,0:T(8,128)(2,1)} %param.20) | copy-start | bytes 1769476
  195.1 7.3 copy-start.10
  195.1 7.3 copy-start.16
  197.8 4.6 collective-permute-start
  203.4 26.0 %copy-start.2 = (f32[1536,768]{1,0:T(8,128)}, f32[1536,768]{1,0:T(8,128)S(1)}, u32[]{:S(2)}) copy-start(f32[1536,768]{1,0:T(8,128)S(1)} %get-tuple-element.64) | copy-start | bytes 14155780
  204.2 25.2 %copy-start.39 = (bf16[1536,768]{1,0:T(8,128)(2,1)S(1)}, bf16[1536,768]{1,0:T(8,128)(2,1)}, u32[]{:S(2)}) copy-start(bf16[1536,768]{1,0:T(8,128)(2,1)} %param.24) | copy-start | bytes 7077892
  229.4 5.0 copy-start.45
  229.4 5.2 copy-start.18
  234.4 4.9 collective-permute-start.1
  245.0 4.6 copy-start.36
  249.6 4.4 copy-start.40
  249.6 28.6 %slice-start = ((s8[4718592]{0:T(1024)(128)(4,1)}), s8[4194304]{0:T(1024)(128)(4,1)S(1)}, s32[]{:S(2)}) async-start(s8[4718592]{0:T(1024)(128)(4,1)} %bitcast.134), calls=%async_computation.8 | async-start | bytes 8388608
  254.0 24.3 %copy-start.5 = (f32[1536,768]{1,0:T(8,128)}, f32[1536,768]{1,0:T(8,128)S(1)}, u32[]{:S(2)}) copy-start(f32[1536,768]{1,0:T(8,128)S(1)} %get-tuple-element.58) | copy-start | bytes 14155780
  254.0 24.3 %copy-start.26 = (f32[1536]{0:T(1024)}, f32[1536]{0:T(1024)S(1)}, u32[]{:S(2)}) copy-start(f32[1536]{0:T(1024)S(1)} %negate_multiply_fusion.2) | copy-start | bytes 18436
  254.0 24.3 %slice-start.1 = ((s8[4718592]{0:T(1024)(128)(4,1)}), s8[524288]{0:T(1024)(128)(4,1)S(1)}, s32[]{:S(2)}) async-start(s8[4718592]{0:T(1024)(128)(4,1)} %bitcast.134), calls=%async_computation.9 | async-start | bytes 1048576
  273.6 4.6 collective-permute-start.2
  281.9 4.9 copy-start.43
  372.4 37.6 %all-to-all-start.3 = ((bf16[16,3,64,256]{3,2,1,0:T(8,128)(2,1)}), bf16[16,3,64,256]{3,2,1,0:T(8,128)(2,1)S(1)}, u32[]{:S(2)}, u32[]{:S(2)}) async-start(bf16[16,3,64,256]{3,2,1,0:T(8,128)(2,1)} %copy.77), calls=%async_computation.3 | async-start | bytes 3145728 | tf_op jit(solution)/shard_map/all_to_all | solution.py:445
  412.7 6.1 slice-start.2
  416.0 3.6 slice-start.3
  426.5 10.0 %copy-start.14 = (bf16[2,6,1,64,256]{4,0,3,1,2:T(2,128)(2,1)S(1)}, bf16[2,6,1,64,256]{4,0,3,1,2:T(2,128)(2,1)}, u32[]{:S(2)}) copy-start(bf16[2,6,1,64,256]{4,0,3,1,2:T(2,128)(2,1)} %copy-done.13) | copy-start | bytes 1179652
  426.5 10.2 %copy-start.25 = (f32[768]{0:T(1024)S(1)}, f32[768]{0:T(1024)}, u32[]{:S(2)}) copy-start(f32[768]{0:T(1024)} %param.21) | copy-start | bytes 9220
  426.5 10.2 %copy-start.38 = (f32[768]{0:T(1024)S(1)}, f32[768]{0:T(1024)}, u32[]{:S(2)}) copy-start(f32[768]{0:T(1024)} %param.22) | copy-start | bytes 9220
  428.9 44.5 %all-to-all-start.4 = ((bf16[16,72,768]{2,1,0:T(8,128)(2,1)}), bf16[16,72,768]{2,1,0:T(8,128)(2,1)}, u32[]{:S(2)}, u32[]{:S(2)}) async-start(bf16[16,72,768]{2,1,0:T(8,128)(2,1)} %convert_element_type.186), calls=%async_computation.4 | async-start | bytes 3538944 | tf_op jit(solution)/shard_map/all_to_all | solution.py:384
  436.7 13.2 %copy-start.27 = (f32[1536]{0:T(1024)S(1)}, f32[1536]{0:T(1024)}, u32[]{:S(2)}) copy-start(f32[1536]{0:T(1024)} %copy-done.26) | copy-start | bytes 18436
  446.3 11.6 %slice-start.4 = ((s8[4718592]{0:T(1024)(128)(4,1)}), s8[524288]{0:T(1024)(128)(4,1)S(1)}, s32[]{:S(2)}) async-start(s8[4718592]{0:T(1024)(128)(4,1)} %bitcast.143), calls=%async_computation.12 | async-start | bytes 1048576
  449.9 8.0 %slice-start.5 = ((s8[4718592]{0:T(1024)(128)(4,1)}), s8[4194304]{0:T(1024)(128)(4,1)S(1)}, s32[]{:S(2)}) async-start(s8[4718592]{0:T(1024)(128)(4,1)} %bitcast.143), calls=%async_computation.13 | async-start | bytes 8388608
  449.9 8.0 %copy-start.29 = (f32[1536]{0:T(1024)S(1)}, f32[1536]{0:T(1024)}, u32[]{:S(2)}) copy-start(f32[1536]{0:T(1024)} %copy-done.28) | copy-start | bytes 18436
  449.9 8.0 %copy-start.41 = (bf16[6,64,1024]{2,1,0:T(8,128)(2,1)S(1)}, bf16[6,64,1024]{2,1,0:T(8,128)(2,1)}, u32[]{:S(2)}) copy-start(bf16[6,64,1024]{2,1,0:T(8,128)(2,1)} %get-tuple-element.28) | copy-start | bytes 2359300
  473.4 113.2 %all-to-all-start.5 = ((bf16[16,216,768]{2,1,0:T(8,128)(2,1)}), bf16[16,216,768]{2,1,0:T(8,128)(2,1)}, u32[]{:S(2)}, u32[]{:S(2)}) async-start(bf16[16,216,768]{2,1,0:T(8,128)(2,1)} %pad_maximum_fusion), calls=%async_computation.5 | async-start | bytes 10616832 | tf_op jit(solution)/shard_map/all_to_all | solution.py:384
  481.6 265.6 %all-gather.5.cloned.1.call-start = ((), (), s32[]{:S(2)}) async-start(), calls=%async_computation.6 | async-start | bytes 1880064 | tf_op jit(solution)/shard_map/all_gather | solution.py:386
  484.0 271.2 %all-gather.7.cloned.1.call-start = ((), (), s32[]{:S(2)}) async-start(), calls=%async_computation.7 | async-start | bytes 5640192 | tf_op jit(solution)/shard_map/all_gather | solution.py:386
  590.8 7.4 copy-start.8
  598.2 133.4 %collective-permute-start.3 = (bf16[1536,768]{1,0:T(8,128)(2,1)}, bf16[1536,768]{1,0:T(8,128)(2,1)}, u32[]{:S(2)}, u32[]{:S(2)}) collective-permute-start(bf16[1536,768]{1,0:T(8,128)(2,1)} %convolution_convert_fusion.3), channel_id=1, source_target_pairs={{0,1},{1,0},{2,3},{3,2},{4,5},{5,4},{6,7},{7,6},{8,9},{9,8},{10,11... | collective-permute-start | bytes 7077896 | tf_op jit(solution)/shard_map/ppermute | solution.py:377
  609.8 10.1 %copy-start.21 = (f32[256,512]{1,0:T(8,128)S(1)}, f32[256,512]{1,0:T(8,128)}, u32[]{:S(2)}) copy-start(f32[256,512]{1,0:T(8,128)} %get-tuple-element.40) | copy-start | bytes 1572868
  617.5 9.1 %copy-start.31 = (f32[768]{0:T(1024)S(1)}, f32[768]{0:T(1024)}, u32[]{:S(2)}) copy-start(f32[768]{0:T(1024)} %get-tuple-element.43) | copy-start | bytes 9220
  617.5 9.1 %copy-start.32 = (f32[768]{0:T(1024)S(1)}, f32[768]{0:T(1024)}, u32[]{:S(2)}) copy-start(f32[768]{0:T(1024)} %get-tuple-element.46) | copy-start | bytes 9220
  617.5 9.1 %copy-start.33 = (f32[768]{0:T(1024)S(1)}, f32[768]{0:T(1024)}, u32[]{:S(2)}) copy-start(f32[768]{0:T(1024)} %get-tuple-element.41) | copy-start | bytes 9220
  617.5 9.1 %copy-start.34 = (f32[768]{0:T(1024)S(1)}, f32[768]{0:T(1024)}, u32[]{:S(2)}) copy-start(f32[768]{0:T(1024)} %get-tuple-element.45) | copy-start | bytes 9220
  764.7 6.2 copy-start.1
  (19 other events, 37.5 us)
Sparse Core Ops, SparseCore 0:
  485.8 119.4 all-gather.4
  608.6 97.2 all-gather.6

commit v2 on v1

v2 whole, which is shorter than its diff:
```python
import math

import jax
import jax.numpy as jnp
from jax import lax
from jax.experimental import pallas as pl
from jax.experimental.pallas import tpu as pltpu
from jax.sharding import PartitionSpec as P

TAU = 8
CONV_WIDTH = 33
HALF_WIDTH = 16
GROUP = 16
PIECE = 256
ITEMS = 2
REACH = 128

COS_SCALE = 0.98
EPS_UNIT = 1e-06
EPS_NORM = 1e-05
NEAR_POLY = (1.158024787902832, -0.36302468180656433, 0.09245320409536362, -0.011449637822806835)
TAIL_POLY = tuple(
    0.5 * a for a in (0.254829592, -0.284496736, 1.421413741, -1.453152027, 1.061405429)
)
SLOPE_SCALE = TAU / math.pi
VMEM_BYTES = 60 * 2**20

F32 = jnp.float32
BF16 = jnp.bfloat16


def norm_terms(values):
    centered = values - jnp.mean(values, axis=-1, keepdims=True)
    inverse = lax.rsqrt(jnp.mean(centered * centered, axis=-1, keepdims=True) + EPS_NORM)
    return centered * inverse, inverse


def norm_back(scaled, unit, inverse):
    along = jnp.mean(scaled * unit, axis=-1, keepdims=True)
    return inverse * (scaled - jnp.mean(scaled, axis=-1, keepdims=True) - unit * along)


def gelu_terms(values):
    share = 1.0 / (1.0 + (0.3275911 * math.sqrt(0.5)) * jnp.abs(values))
    bell = jnp.exp(-0.5 * (values * values))
    poly = TAIL_POLY[4] * share + TAIL_POLY[3]
    for coefficient in TAIL_POLY[2::-1]:
        poly = poly * share + coefficient
    tail = poly * (share * bell)
    below = jnp.where(values < 0.0, tail, 1.0 - tail)
    return values * below, below + values * (bell * (1.0 / math.sqrt(2.0 * math.pi)))


def place_of_item(rows):
    item_at = lax.broadcasted_iota(jnp.int32, (rows, rows), 0)
    place_at = lax.broadcasted_iota(jnp.int32, (rows, rows), 1)
    hit = item_at == (place_at & 1) * PIECE + (place_at >> 1)
    return jnp.where(hit, 1.0, 0.0).astype(BF16)


def lasting(microseconds):
    return pl.CostEstimate(flops=microseconds * 1_150_000_000, bytes_accessed=0, transcendentals=0)


def contract(left, right, left_dim, right_dim):
    return lax.dot_general(
        left, right, (((left_dim,), (right_dim,)), ((), ())), preferred_element_type=F32
    )


def pair_terms(dots, same=None):
    upper = 1.0 / COS_SCALE + dots
    lower = 1.0 / COS_SCALE - dots
    upper_inv = lax.rsqrt(upper)
    lower_inv = lax.rsqrt(lower)
    wide = 1.0 / 0.7 + lower * lower_inv
    wide_inv = lax.rsqrt(wide)
    root = wide * wide_inv
    ratio = NEAR_POLY[3] * root + NEAR_POLY[2]
    ratio = ratio * root + NEAR_POLY[1]
    ratio = ratio * root + NEAR_POLY[0]
    near = ratio * ((upper * upper_inv) * wide_inv)
    if same is not None:
        near = jnp.where(same, near, 0.0)
    near_2 = near * near
    near_4 = near_2 * near_2
    weights = (near_4 * near_4).astype(BF16)
    slopes = ((near_4 * near_2) * (near * (upper_inv * lower_inv))).astype(BF16)
    return weights, slopes


def banded(line):
    return pltpu.roll(
        jnp.broadcast_to(line, (PIECE, line.shape[1])), 0, 1, stride=1, stride_axis=0
    )


def reversed_rows(columns):
    at = lax.broadcasted_iota(jnp.int32, (PIECE, PIECE), 0)
    to = lax.broadcasted_iota(jnp.int32, (PIECE, PIECE), 1)
    flip = jnp.where(at + to == PIECE - 1, 1.0, 0.0).astype(BF16)
    return contract(flip, columns, 1, 1).astype(BF16)


def unbanded(products):
    wide = products.shape[1]
    turned = pltpu.roll(products, wide - (PIECE - 1), 1, stride=1, stride_axis=0)
    return jnp.sum(turned, axis=0, keepdims=True)


def pad_lanes(dst, src, length):
    dst[:, pl.ds(0, REACH)] = jnp.zeros((dst.shape[0], REACH), dst.dtype)
    dst[:, pl.ds(REACH, length)] = src
    dst[:, pl.ds(REACH + length, REACH)] = jnp.zeros((dst.shape[0], REACH), dst.dtype)


def rows_of(dst, src, length):
    for start in range(0, length, PIECE):
        dst[pl.ds(start, PIECE), :] = src[:, pl.ds(start, PIECE)].T


def long_forward(query, key, value, line):
    head_dim, length = query.shape
    blocks = length // PIECE
    step = 512

    def body(q_ref, k_ref, v_ref, line_ref, o_ref, w_ref, s_ref, key_rows, value_pad, band_ref):
        block = pl.program_id(0)

        @pl.when(block == 0)
        def _():
            rows_of(key_rows, k_ref, length)
            pad_lanes(value_pad, v_ref[...], length)
            band_ref[...] = banded(line_ref[...]).astype(BF16)

        q = q_ref[...]
        start = pl.multiple_of(block * PIECE, PIECE)
        total = contract(value_pad[:, pl.ds(start, PIECE + 2 * REACH)], band_ref[...], 1, 1)
        for at in range(0, length, step):
            dots = contract(key_rows[pl.ds(at, step), :], q, 1, 0)
            weights, slopes = pair_terms(dots)
            w_ref[pl.ds(at, step), :] = weights
            s_ref[pl.ds(at, step), :] = slopes
            total = total + contract(v_ref[:, pl.ds(at, step)], weights, 1, 0)
        o_ref[...] = total.astype(BF16)

    whole = pl.BlockSpec((head_dim, length), lambda i: (0, 0))
    large = pl.BlockSpec((None, length, PIECE), lambda i: (i, 0, 0))
    large_shape = jax.ShapeDtypeStruct((blocks, length, PIECE), BF16)
    return pl.pallas_call(
        body,
        grid=(blocks,),
        in_specs=[
            pl.BlockSpec((head_dim, PIECE), lambda i: (0, i)),
            whole,
            whole,
            pl.BlockSpec((1, PIECE + 2 * REACH), lambda i: (0, 0)),
        ],
        out_specs=[pl.BlockSpec((None, head_dim, PIECE), lambda i: (i, 0, 0)), large, large],
        out_shape=[jax.ShapeDtypeStruct((blocks, head_dim, PIECE), BF16), large_shape, large_shape],
        scratch_shapes=[
            pltpu.VMEM((length, head_dim), BF16),
            pltpu.VMEM((head_dim, length + 2 * REACH), BF16),
            pltpu.VMEM((PIECE, PIECE + 2 * REACH), BF16),
        ],
        compiler_params=pltpu.CompilerParams(vmem_limit_bytes=VMEM_BYTES),
        cost_estimate=lasting(70),
    )(query, key, value, line)


def long_back_values(value, grad, line, weights):
    head_dim, length = value.shape
    blocks = length // PIECE
    step = 1024
    wide = PIECE + 2 * REACH

    def body(
        v_ref, g_ref, line_ref, w_ref, dv_ref, taps_ref,
        value_pad, grad_pad, value_sum, band_ref, products,
    ):
        block = pl.program_id(0)

        @pl.when(block == 0)
        def _():
            pad_lanes(value_pad, v_ref[...], length)
            pad_lanes(grad_pad, g_ref[...], length)
            value_sum[...] = jnp.zeros_like(value_sum)
            products[...] = jnp.zeros_like(products)
            band_ref[...] = banded(line_ref[...]).astype(BF16)

        start = pl.multiple_of(block * PIECE, PIECE)
        g = g_ref[:, pl.ds(start, PIECE)]
        near_values = value_pad[:, pl.ds(start, wide)]
        near_grads = grad_pad[:, pl.ds(start, wide)]
        products[...] += contract(reversed_rows(g), near_values, 1, 0)
        value_sum[:, pl.ds(start, PIECE)] += contract(near_grads, band_ref[...], 1, 1)
        for at in range(0, length, step):
            value_sum[:, pl.ds(at, step)] += contract(g, w_ref[pl.ds(at, step), :], 1, 1)

        @pl.when(block == blocks - 1)
        def _():
            for index in range(blocks):
                dv_ref[index] = value_sum[:, pl.ds(index * PIECE, PIECE)].astype(BF16)
            taps_ref[...] = unbanded(products[...])

    whole = pl.BlockSpec((head_dim, length), lambda i: (0, 0))
    return pl.pallas_call(
        body,
        grid=(blocks,),
        in_specs=[
            whole,
            whole,
            pl.BlockSpec((1, wide), lambda i: (0, 0)),
            pl.BlockSpec((None, length, PIECE), lambda i: (i, 0, 0)),
        ],
        out_specs=[
            pl.BlockSpec((blocks, head_dim, PIECE), lambda i: (0, 0, 0)),
            pl.BlockSpec((1, wide), lambda i: (0, 0)),
        ],
        out_shape=[
            jax.ShapeDtypeStruct((blocks, head_dim, PIECE), BF16),
            jax.ShapeDtypeStruct((1, wide), F32),
        ],
        scratch_shapes=[
            pltpu.VMEM((head_dim, length + 2 * REACH), BF16),
            pltpu.VMEM((head_dim, length + 2 * REACH), BF16),
            pltpu.VMEM((head_dim, length), F32),
            pltpu.VMEM((PIECE, wide), BF16),
            pltpu.VMEM((PIECE, wide), F32),
        ],
        compiler_params=pltpu.CompilerParams(vmem_limit_bytes=VMEM_BYTES),
        cost_estimate=lasting(16),
    )(value, grad, line, weights)


def long_back_pairs(query, key, value, grad, slopes):
    head_dim, length = query.shape
    blocks = length // PIECE
    step = 1024

    def body(q_ref, k_ref, v_ref, g_ref, s_ref, dq_ref, dk_ref, value_rows, key_sum):
        block = pl.program_id(0)

        @pl.when(block == 0)
        def _():
            rows_of(value_rows, v_ref, length)
            key_sum[...] = jnp.zeros_like(key_sum)

        q = q_ref[...]
        g = g_ref[...]
        total = jnp.zeros((head_dim, PIECE), F32)
        for at in range(0, length, step):
            grad_weights = contract(value_rows[pl.ds(at, step), :], g, 1, 0)
            terms = grad_weights.astype(BF16) * s_ref[pl.ds(at, step), :]
            total = total + contract(k_ref[:, pl.ds(at, step)], terms, 1, 0)
            key_sum[:, pl.ds(at, step)] += contract(q, terms, 1, 1)
        dq_ref[...] = (total * SLOPE_SCALE).astype(BF16)

        @pl.when(block == blocks - 1)
        def _():
            for index in range(blocks):
                piece = key_sum[:, pl.ds(index * PIECE, PIECE)]
                dk_ref[index] = (piece * SLOPE_SCALE).astype(BF16)

    whole = pl.BlockSpec((head_dim, length), lambda i: (0, 0))
    piece = pl.BlockSpec((head_dim, PIECE), lambda i: (0, i))
    pieces_shape = jax.ShapeDtypeStruct((blocks, head_dim, PIECE), BF16)
    return pl.pallas_call(
        body,
        grid=(blocks,),
        in_specs=[
            piece,
            whole,
            whole,
            piece,
            pl.BlockSpec((None, length, PIECE), lambda i: (i, 0, 0)),
        ],
        out_specs=[
            pl.BlockSpec((None, head_dim, PIECE), lambda i: (i, 0, 0)),
            pl.BlockSpec((blocks, head_dim, PIECE), lambda i: (0, 0, 0)),
        ],
        out_shape=[pieces_shape] * 2,
        scratch_shapes=[
            pltpu.VMEM((length, head_dim), BF16),
            pltpu.VMEM((head_dim, length), F32),
        ],
        compiler_params=pltpu.CompilerParams(vmem_limit_bytes=VMEM_BYTES),
        cost_estimate=lasting(40),
    )(query, key, value, grad, slopes)


def short_forward(reach, ids_row, ids_col, pack, line):
    _, heads, head_dim, length = pack.shape
    blocks = length // PIECE
    wide = PIECE + 2 * REACH

    def body(
        reach_ref, row_ref, col_ref, q_ref, k_ref, v_ref, line_ref,
        o_ref, w_ref, s_ref, key_rows, value_pad, total, band_ref,
    ):
        block = pl.program_id(0)

        @pl.when(block == 0)
        def _():
            for h in range(heads):
                rows_of(key_rows.at[h], k_ref.at[h], length)
                pad_lanes(value_pad.at[h], v_ref[h], length)
                band_ref[h] = banded(line_ref[h])

        start = pl.multiple_of(block * PIECE, PIECE)
        near = (col_ref[pl.ds(start, PIECE), :] == row_ref[:, pl.ds(start, wide)]).astype(F32)
        for h in range(heads):
            masked = (band_ref[h] * near).astype(BF16)
            total[h] = contract(value_pad[h, :, pl.ds(start, wide)], masked, 1, 1)

        own_ids = row_ref[:, pl.ds(start + REACH, PIECE)]

        def turn(step, carry):
            at = pl.multiple_of(step * PIECE, PIECE)
            same = col_ref[pl.ds(at, PIECE), :] == own_ids
            for h in range(heads):
                dots = contract(key_rows[h, pl.ds(at, PIECE), :], q_ref[h], 1, 0)
                weights, slopes = pair_terms(dots, same)
                w_ref[h, pl.ds(at, PIECE), :] = weights
                s_ref[h, pl.ds(at, PIECE), :] = slopes
                total[h] += contract(v_ref[h, :, pl.ds(at, PIECE)], weights, 1, 0)
            return carry

        lax.fori_loop(reach_ref[0, block], reach_ref[1, block], turn, 0)
        o_ref[...] = total[...].astype(BF16)

    def packed(which):
        return pl.BlockSpec((None, heads, head_dim, length), lambda i: (which, 0, 0, 0))

    block_spec = pl.BlockSpec((heads, head_dim, PIECE), lambda i: (0, 0, i))
    large = pl.BlockSpec((None, heads, length, PIECE), lambda i: (i, 0, 0, 0))
    large_shape = jax.ShapeDtypeStruct((blocks, heads, length, PIECE), BF16)
    return pl.pallas_call(
        body,
        grid=(blocks,),
        in_specs=[
            pl.BlockSpec(memory_space=pltpu.SMEM),
            pl.BlockSpec((1, length + 2 * REACH), lambda i: (0, 0)),
            pl.BlockSpec((length, 1), lambda i: (0, 0)),
            pl.BlockSpec((None, heads, head_dim, PIECE), lambda i: (0, 0, 0, i)),
            packed(1),
            packed(2),
            pl.BlockSpec((heads, 1, wide), lambda i: (0, 0, 0)),
        ],
        out_specs=[block_spec, large, large],
        out_shape=[jax.ShapeDtypeStruct((heads, head_dim, length), BF16), large_shape, large_shape],
        scratch_shapes=[
            pltpu.VMEM((heads, length, head_dim), BF16),
            pltpu.VMEM((heads, head_dim, length + 2 * REACH), BF16),
            pltpu.VMEM((heads, head_dim, PIECE), F32),
            pltpu.VMEM((heads, PIECE, wide), F32),
        ],
        compiler_params=pltpu.CompilerParams(vmem_limit_bytes=VMEM_BYTES),
        cost_estimate=lasting(28),
    )(reach, ids_row, ids_col, pack, pack, pack, line)


def short_backward(
    part, parts, reach, ids_row, ids_col, pack, grad, line, weights, slopes
):
    _, all_heads, head_dim, length = pack.shape
    heads = all_heads // parts
    blocks = length // PIECE
    wide = PIECE + 2 * REACH

    def body(
        reach_ref, row_ref, col_ref, q_ref, k_ref, v_ref, g_ref, line_ref, w_ref, s_ref,
        dq_ref, dk_ref, dv_ref, taps_ref, value_rows, value_pad, grad_pad, band_ref, products,
    ):
        block = pl.program_id(0)

        @pl.when(block == 0)
        def _():
            for h in range(heads):
                rows_of(value_rows.at[h], v_ref.at[h], length)
                pad_lanes(value_pad.at[h], v_ref[h], length)
                pad_lanes(grad_pad.at[h], g_ref[h], length)
                band_ref[h] = banded(line_ref[h])
            dk_ref[...] = jnp.zeros_like(dk_ref)
            dv_ref[...] = jnp.zeros_like(dv_ref)
            products[...] = jnp.zeros_like(products)

        start = pl.multiple_of(block * PIECE, PIECE)
        near = (col_ref[pl.ds(start, PIECE), :] == row_ref[:, pl.ds(start, wide)]).astype(F32)
        at = lax.broadcasted_iota(jnp.int32, (PIECE, PIECE), 0)
        to = lax.broadcasted_iota(jnp.int32, (PIECE, PIECE), 1)
        flip = jnp.where(at + to == PIECE - 1, 1.0, 0.0).astype(BF16)
        near_flip = contract(flip, near.astype(BF16), 1, 0)
        for h in range(heads):
            masked = (band_ref[h] * near).astype(BF16)
            own = g_ref[h, :, pl.ds(start, PIECE)]
            products[h] += (
                contract(reversed_rows(own), value_pad[h, :, pl.ds(start, wide)], 1, 0) * near_flip
            )
            dv_ref[h, :, pl.ds(start, PIECE)] += contract(
                grad_pad[h, :, pl.ds(start, wide)], masked, 1, 1
            )
        dq_ref[...] = jnp.zeros_like(dq_ref)

        def turn(step, carry):
            at = pl.multiple_of(step * PIECE, PIECE)
            for h in range(heads):
                own = g_ref[h, :, pl.ds(start, PIECE)]
                grad_weights = contract(value_rows[h, pl.ds(at, PIECE), :], own, 1, 0)
                terms = grad_weights.astype(BF16) * s_ref[h, pl.ds(at, PIECE), :]
                dq_ref[h] += contract(k_ref[h, :, pl.ds(at, PIECE)], terms, 1, 0) * SLOPE_SCALE
                dk_ref[h, :, pl.ds(at, PIECE)] += contract(q_ref[h], terms, 1, 1) * SLOPE_SCALE
                dv_ref[h, :, pl.ds(at, PIECE)] += contract(own, w_ref[h, pl.ds(at, PIECE), :], 1, 1)
            return carry

        lax.fori_loop(reach_ref[0, block], reach_ref[1, block], turn, 0)

        @pl.when(block == blocks - 1)
        def _():
            for h in range(heads):
                taps_ref[h] = unbanded(products[h])

    def packed(which):
        return pl.BlockSpec((None, heads, head_dim, length), lambda i: (which, part, 0, 0))

    whole = pl.BlockSpec((heads, head_dim, length), lambda i: (0, 0, 0))
    large = pl.BlockSpec((None, heads, length, PIECE), lambda i: (i, part, 0, 0))
    whole_shape = jax.ShapeDtypeStruct((heads, head_dim, length), F32)
    return pl.pallas_call(
        body,
        grid=(blocks,),
        in_specs=[
            pl.BlockSpec(memory_space=pltpu.SMEM),
            pl.BlockSpec((1, length + 2 * REACH), lambda i: (0, 0)),
            pl.BlockSpec((length, 1), lambda i: (0, 0)),
            pl.BlockSpec((None, heads, head_dim, PIECE), lambda i: (0, part, 0, i)),
            packed(1),
            packed(2),
            pl.BlockSpec((heads, head_dim, length), lambda i: (part, 0, 0)),
            pl.BlockSpec((heads, 1, wide), lambda i: (part, 0, 0)),
            large,
            large,
        ],
        out_specs=[
            pl.BlockSpec((heads, head_dim, PIECE), lambda i: (0, 0, i)),
            whole,
            whole,
            pl.BlockSpec((heads, 1, wide), lambda i: (0, 0, 0)),
        ],
        out_shape=[whole_shape] * 3 + [jax.ShapeDtypeStruct((heads, 1, wide), F32)],
        scratch_shapes=[
            pltpu.VMEM((heads, length, head_dim), BF16),
            pltpu.VMEM((heads, head_dim, length + 2 * REACH), BF16),
            pltpu.VMEM((heads, head_dim, length + 2 * REACH), BF16),
            pltpu.VMEM((heads, PIECE, wide), F32),
            pltpu.VMEM((heads, PIECE, wide), F32),
        ],
        compiler_params=pltpu.CompilerParams(vmem_limit_bytes=VMEM_BYTES),
        cost_estimate=lasting(28),
    )(reach, ids_row, ids_col, pack, pack, pack, grad, line, weights, slopes)


def project_in(tokens, query_weight, key_weight, value_weight, heads):
    row_total, width = tokens.shape
    cols = query_weight.shape[1]
    head_dim = cols // heads
    blocks = row_total // PIECE
    long_rows = ITEMS * PIECE

    def body(t_ref, wq_ref, wk_ref, wv_ref, long_ref, short_ref, unit_ref, inv_ref, turned, rows):
        block = pl.program_id(0)

        @pl.when(block == 0)
        def _():
            for index, ref in enumerate((wq_ref, wk_ref, wv_ref)):
                turned[pl.ds(index * cols, cols), :] = ref[...].T
            long_ref[pl.ds(ITEMS * heads, GROUP - ITEMS * heads)] = jnp.zeros(
                (GROUP - ITEMS * heads, 3 * head_dim, PIECE), BF16
            )

        @pl.when(block < ITEMS)
        def _():
            item_at = lax.broadcasted_iota(jnp.int32, (PIECE, long_rows), 0)
            place_at = lax.broadcasted_iota(jnp.int32, (PIECE, long_rows), 1)
            pick = jnp.where(place_at == ITEMS * item_at + block, 1.0, 0.0).astype(BF16)
            rows[...] = contract(pick, t_ref[pl.ds(0, long_rows), :], 1, 0).astype(BF16)

        @pl.when(block >= ITEMS)
        def _():
            rows[...] = t_ref[pl.ds(pl.multiple_of(block * PIECE, PIECE), PIECE), :]

        parts = contract(turned[...], rows[...], 1, 1).reshape(3, heads, head_dim, PIECE)
        raw = parts[:2]
        inverse = lax.rsqrt(jnp.sum(raw * raw, axis=2, keepdims=True) + EPS_UNIT)
        unit = raw * inverse
        unit_ref[...] = unit
        inv_ref[...] = inverse
        low = unit.astype(BF16)
        short_ref[:2] = low
        short_ref[2] = parts[2].astype(BF16)

        @pl.when(block < ITEMS)
        def _():
            for h in range(heads):
                unit_at = block * heads + h
                long_ref[unit_at, pl.ds(0, head_dim), :] = low[0, h]
                long_ref[unit_at, pl.ds(head_dim, head_dim), :] = low[1, h]
                long_ref[unit_at, pl.ds(2 * head_dim, head_dim), :] = parts[2, h].astype(BF16)

    weight = pl.BlockSpec((width, cols), lambda i: (0, 0))
    return pl.pallas_call(
        body,
        grid=(blocks,),
        in_specs=[pl.BlockSpec((row_total, width), lambda i: (0, 0)), weight, weight, weight],
        out_specs=[
            pl.BlockSpec((GROUP, 3 * head_dim, PIECE), lambda i: (0, 0, 0)),
            pl.BlockSpec(
                (3, heads, head_dim, PIECE), lambda i: (0, 0, 0, jnp.maximum(i - ITEMS, 0))
            ),
            pl.BlockSpec((2, heads, head_dim, PIECE), lambda i: (0, 0, 0, i)),
            pl.BlockSpec((2, heads, 1, PIECE), lambda i: (0, 0, 0, i)),
        ],
        out_shape=[
            jax.ShapeDtypeStruct((GROUP, 3 * head_dim, PIECE), BF16),
            jax.ShapeDtypeStruct((3, heads, head_dim, row_total - long_rows), BF16),
            jax.ShapeDtypeStruct((2, heads, head_dim, row_total), F32),
            jax.ShapeDtypeStruct((2, heads, 1, row_total), F32),
        ],
        scratch_shapes=[pltpu.VMEM((3 * cols, width), BF16), pltpu.VMEM((PIECE, width), BF16)],
        compiler_params=pltpu.CompilerParams(vmem_limit_bytes=VMEM_BYTES),
        cost_estimate=lasting(10),
    )(tokens, query_weight, key_weight, value_weight)


def project_out(moved, short_att, out_weight):
    heads, head_dim, short_rows = short_att.shape
    cols, width = out_weight.shape
    span = ITEMS * PIECE
    blocks = 1 + short_rows // span

    def body(m_ref, a_ref, w_ref, mixed_ref, part_ref, items):
        block = pl.program_id(0)

        @pl.when(block == 0)
        def _():
            for h in range(heads):
                for item in range(ITEMS):
                    items[pl.ds(h * head_dim, head_dim), pl.ds(item * PIECE, PIECE)] = m_ref[
                        item * heads + h
                    ]
            mixed_ref[...] = contract(items[...], place_of_item(span), 1, 0).astype(BF16)

        @pl.when(block > 0)
        def _():
            mixed_ref[...] = a_ref[...].reshape(cols, span)

        part_ref[...] = contract(mixed_ref[...], w_ref[...], 0, 0).astype(BF16)

    return pl.pallas_call(
        body,
        grid=(blocks,),
        in_specs=[
            pl.BlockSpec((GROUP, head_dim, PIECE), lambda i: (0, 0, 0)),
            pl.BlockSpec((heads, head_dim, span), lambda i: (0, 0, jnp.maximum(i - 1, 0))),
            pl.BlockSpec((cols, width), lambda i: (0, 0)),
        ],
        out_specs=[
            pl.BlockSpec((cols, span), lambda i: (0, i)),
            pl.BlockSpec((span, width), lambda i: (i, 0)),
        ],
        out_shape=[
            jax.ShapeDtypeStruct((cols, span * blocks), BF16),
            jax.ShapeDtypeStruct((span * blocks, width), BF16),
        ],
        scratch_shapes=[pltpu.VMEM((cols, span), BF16)],
        compiler_params=pltpu.CompilerParams(vmem_limit_bytes=VMEM_BYTES),
        cost_estimate=lasting(5),
    )(moved, short_att, out_weight)


def feed_forward(tokens, own, other, gain, bias, inner_weight, outer_weight):
    row_total, width = tokens.shape
    hidden_units = inner_weight.shape[1]

    def body(
        t_ref, own_ref, other_ref, gain_ref, bias_ref, inner_ref, outer_ref,
        unit_ref, inv_ref, low_ref, act_ref, slope_ref, part_ref,
    ):
        hidden = t_ref[...].astype(F32) + (
            own_ref[...].astype(F32) + other_ref[...].astype(F32)
        )
        unit, inverse = norm_terms(hidden)
        unit_ref[...] = unit
        inv_ref[...] = inverse
        low = (unit * gain_ref[...] + bias_ref[...]).astype(BF16)
        low_ref[...] = low
        act, slope = gelu_terms(contract(low, inner_ref[...], 1, 0))
        act = act.astype(BF16)
        act_ref[...] = act
        slope_ref[...] = slope.astype(BF16)
        part_ref[...] = contract(act, outer_ref[...], 1, 0).astype(BF16)

    rows = pl.BlockSpec((PIECE, width), lambda i: (i, 0))
    units = pl.BlockSpec((PIECE, hidden_units), lambda i: (i, 0))
    line = pl.BlockSpec((1, width), lambda i: (0, 0))
    return pl.pallas_call(
        body,
        grid=(row_total // PIECE,),
        in_specs=[
            rows, rows, rows, line, line,
            pl.BlockSpec((width, hidden_units), lambda i: (0, 0)),
            pl.BlockSpec((hidden_units, width), lambda i: (0, 0)),
        ],
        out_specs=[rows, pl.BlockSpec((PIECE, 1), lambda i: (i, 0)), rows, units, units, rows],
        out_shape=[
            jax.ShapeDtypeStruct((row_total, width), F32),
            jax.ShapeDtypeStruct((row_total, 1), F32),
            jax.ShapeDtypeStruct((row_total, width), BF16),
            jax.ShapeDtypeStruct((row_total, hidden_units), BF16),
            jax.ShapeDtypeStruct((row_total, hidden_units), BF16),
            jax.ShapeDtypeStruct((row_total, width), BF16),
        ],
        compiler_params=pltpu.CompilerParams(vmem_limit_bytes=VMEM_BYTES),
        cost_estimate=lasting(20),
    )(tokens, own, other, gain, bias, inner_weight, outer_weight)


def feed_back(
    unit_one, own, other, gain_one, bias_one, gain_two, bias_two, cotangent, slope,
    inner_weight, outer_weight,
):
    row_total, width = unit_one.shape
    hidden_units = inner_weight.shape[1]

    def body(
        unit_ref, own_ref, other_ref, gain_one_ref, bias_one_ref, gain_ref, bias_ref, g_ref,
        slope_ref, inner_ref, outer_ref,
        out_ref, sum_ref, low_ref, pre_ref, part_ref, gain_grad_ref, bias_grad_ref,
    ):
        @pl.when(pl.program_id(0) == 0)
        def _():
            gain_grad_ref[...] = jnp.zeros_like(gain_grad_ref)
            bias_grad_ref[...] = jnp.zeros_like(bias_grad_ref)

        normed = unit_ref[...] * gain_one_ref[...] + bias_one_ref[...]
        unit, inverse = norm_terms(
            normed + (own_ref[...].astype(F32) + other_ref[...].astype(F32))
        )
        out_ref[...] = (unit * gain_ref[...] + bias_ref[...]).astype(BF16)
        g = g_ref[...].astype(F32)
        gain_grad_ref[...] += jnp.sum(g * unit, axis=0, keepdims=True)
        bias_grad_ref[...] += jnp.sum(g, axis=0, keepdims=True)
        grad_sum = norm_back(g * gain_ref[...], unit, inverse)
        sum_ref[...] = grad_sum
        low = grad_sum.astype(BF16)
        low_ref[...] = low
        pre = contract(low, outer_ref[...], 1, 1) * slope_ref[...].astype(F32)
        pre = pre.astype(BF16)
        pre_ref[...] = pre
        part_ref[...] = contract(pre, inner_ref[...], 1, 1).astype(BF16)

    rows = pl.BlockSpec((PIECE, width), lambda i: (i, 0))
    units = pl.BlockSpec((PIECE, hidden_units), lambda i: (i, 0))
    line = pl.BlockSpec((1, width), lambda i: (0, 0))
    return pl.pallas_call(
        body,
        grid=(row_total // PIECE,),
        in_specs=[
            rows, rows, rows, line, line, line, line, rows, units,
            pl.BlockSpec((width, hidden_units), lambda i: (0, 0)),
            pl.BlockSpec((hidden_units, width), lambda i: (0, 0)),
        ],
        out_specs=[rows, rows, rows, units, rows, line, line],
        out_shape=[
            jax.ShapeDtypeStruct((row_total, width), BF16),
            jax.ShapeDtypeStruct((row_total, width), F32),
            jax.ShapeDtypeStruct((row_total, width), BF16),
            jax.ShapeDtypeStruct((row_total, hidden_units), BF16),
            jax.ShapeDtypeStruct((row_total, width), BF16),
            jax.ShapeDtypeStruct((1, width), F32),
            jax.ShapeDtypeStruct((1, width), F32),
        ],
        compiler_params=pltpu.CompilerParams(vmem_limit_bytes=VMEM_BYTES),
        cost_estimate=lasting(18),
    )(
        unit_one, own, other, gain_one, bias_one, gain_two, bias_two, cotangent, slope,
        inner_weight, outer_weight,
    )


def project_back(unit, inverse, grad_sum, own, other, gain, out_weight, heads):
    row_total, width = unit.shape
    cols = out_weight.shape[0]
    head_dim = cols // heads
    span = ITEMS * PIECE
    blocks = row_total // span

    def body(
        unit_ref, inv_ref, sum_ref, own_ref, other_ref, gain_ref, w_ref,
        hidden_ref, low_ref, long_ref, short_ref, gain_grad_ref, bias_grad_ref,
    ):
        block = pl.program_id(0)

        @pl.when(block == 0)
        def _():
            gain_grad_ref[...] = jnp.zeros_like(gain_grad_ref)
            bias_grad_ref[...] = jnp.zeros_like(bias_grad_ref)

        unit = unit_ref[...]
        grad = sum_ref[...] + (own_ref[...].astype(F32) + other_ref[...].astype(F32))
        gain_grad_ref[...] += jnp.sum(grad * unit, axis=0, keepdims=True)
        bias_grad_ref[...] += jnp.sum(grad, axis=0, keepdims=True)
        hidden = norm_back(grad * gain_ref[...], unit, inv_ref[...])
        hidden_ref[...] = hidden
        low = hidden.astype(BF16)
        low_ref[...] = low
        att = contract(w_ref[...], low, 1, 1).astype(BF16)

        @pl.when(block == 0)
        def _():
            items = contract(att, place_of_item(span), 1, 1).astype(BF16)
            for h in range(heads):
                for item in range(ITEMS):
                    long_ref[item * heads + h] = items[
                        h * head_dim : (h + 1) * head_dim, item * PIECE : (item + 1) * PIECE
                    ]
            long_ref[pl.ds(ITEMS * heads, GROUP - ITEMS * heads)] = jnp.zeros(
                (GROUP - ITEMS * heads, head_dim, PIECE), BF16
            )

        short_ref[...] = att.reshape(heads, head_dim, span)

    rows = pl.BlockSpec((span, width), lambda i: (i, 0))
    line = pl.BlockSpec((1, width), lambda i: (0, 0))
    return pl.pallas_call(
        body,
        grid=(blocks,),
        in_specs=[
            rows, pl.BlockSpec((span, 1), lambda i: (i, 0)), rows, rows, rows, line,
            pl.BlockSpec((cols, width), lambda i: (0, 0)),
        ],
        out_specs=[
            rows,
            rows,
            pl.BlockSpec((GROUP, head_dim, PIECE), lambda i: (0, 0, 0)),
            pl.BlockSpec((heads, head_dim, span), lambda i: (0, 0, jnp.maximum(i - 1, 0))),
            line,
            line,
        ],
        out_shape=[
            jax.ShapeDtypeStruct((row_total, width), F32),
            jax.ShapeDtypeStruct((row_total, width), BF16),
            jax.ShapeDtypeStruct((GROUP, head_dim, PIECE), BF16),
            jax.ShapeDtypeStruct((heads, head_dim, row_total - span), BF16),
            jax.ShapeDtypeStruct((1, width), F32),
            jax.ShapeDtypeStruct((1, width), F32),
        ],
        compiler_params=pltpu.CompilerParams(vmem_limit_bytes=VMEM_BYTES),
        cost_estimate=lasting(12),
    )(unit, inverse, grad_sum, own, other, gain, out_weight)


def unit_back(moved_pairs, moved_values, short_parts, unit, inverse):
    heads, head_dim = unit.shape[1:3]
    short_heads, _, short_rows = short_parts[0][0].shape
    count = len(short_parts)
    span = ITEMS * PIECE
    blocks = 1 + short_rows // span
    cols = heads * head_dim

    def body(*refs):
        pairs_ref, values_ref = refs[:2]
        short_refs = refs[2 : 2 + 3 * count]
        unit_ref, inv_ref, out_ref, items = refs[2 + 3 * count :]
        block = pl.program_id(0)

        def short_part(which):
            return jnp.concatenate([short_refs[3 * at + which][...] for at in range(count)], axis=0)

        def back(which, grad):
            unit = unit_ref[which]
            along = jnp.sum(unit * grad, axis=1, keepdims=True)
            return ((grad - unit * along) * inv_ref[which]).astype(BF16).reshape(cols, span)

        @pl.when(block == 0)
        def _():
            def long_part(ref, at):
                part = pl.ds(at, head_dim)
                heads_of = [
                    jnp.concatenate([ref[h, part, :], ref[heads + h, part, :]], axis=1)
                    for h in range(heads)
                ]
                return jnp.stack(heads_of, axis=0)

            for which in range(2):
                items[pl.ds(which * cols, cols), :] = back(
                    which, long_part(pairs_ref, which * head_dim).astype(F32)
                )
            items[pl.ds(2 * cols, cols), :] = long_part(values_ref, 0).reshape(cols, span)
            out_ref[...] = contract(items[...], place_of_item(span), 1, 0).astype(BF16)

        @pl.when(block > 0)
        def _():
            out_ref[pl.ds(0, cols), :] = back(0, short_part(0))
            out_ref[pl.ds(cols, cols), :] = back(1, short_part(1))
            out_ref[pl.ds(2 * cols, cols), :] = short_part(2).astype(BF16).reshape(
                cols, span
            )

    short = pl.BlockSpec(
        (short_heads, head_dim, span), lambda i: (0, 0, jnp.maximum(i - 1, 0))
    )
    return pl.pallas_call(
        body,
        grid=(blocks,),
        in_specs=[
            pl.BlockSpec((GROUP, moved_pairs.shape[1], PIECE), lambda i: (0, 0, 0)),
            pl.BlockSpec((GROUP, head_dim, PIECE), lambda i: (0, 0, 0)),
        ]
        + [short] * (3 * count)
        + [
            pl.BlockSpec((2, heads, head_dim, span), lambda i: (0, 0, 0, i)),
            pl.BlockSpec((2, heads, 1, span), lambda i: (0, 0, 0, i)),
        ],
        out_specs=pl.BlockSpec((3 * cols, span), lambda i: (0, i)),
        out_shape=jax.ShapeDtypeStruct((3 * cols, span * blocks), BF16),
        scratch_shapes=[pltpu.VMEM((3 * cols, span), BF16)],
        compiler_params=pltpu.CompilerParams(vmem_limit_bytes=VMEM_BYTES),
        cost_estimate=lasting(8),
    )(moved_pairs, moved_values, *sum(map(tuple, short_parts), ()), unit, inverse)


def other_half(part):
    return lax.ppermute(part, "tp", [(0, 1), (1, 0)])


def halves(part, bits, bit):
    mine = (lax.axis_index("seq") >> bit) & 1
    axis = bits.index(bit)
    return tuple(
        lax.dynamic_index_in_dim(part, side, axis, False) for side in (1 - mine, mine)
    )


def across_bit(sent, kept, bit):
    peers = lax.axis_size("seq")
    came = lax.ppermute(sent, "seq", [(i, i ^ (1 << bit)) for i in range(peers)])
    return (kept.astype(F32) + came.astype(F32)).astype(BF16)


def after(first, second):
    return lax.optimization_barrier((first, second))


def shards(
    tokens,
    short_lengths,
    query_weight,
    key_weight,
    value_weight,
    conv_kernel,
    out_weight,
    gain_one,
    bias_one,
    inner_weight,
    outer_weight,
    gain_two,
    bias_two,
    cotangent,
):
    row_total, width = tokens.shape
    heads_dev = conv_kernel.shape[0]
    head_cols = query_weight.shape[1]
    head_dim = head_cols // heads_dev
    short_rows = row_total - ITEMS * PIECE
    units = ITEMS * heads_dev
    place = lax.axis_index("seq") % GROUP
    groups = [
        [first + i for i in range(GROUP)] for first in range(0, lax.axis_size("seq"), GROUP)
    ]

    def exchange(pieces):
        return lax.all_to_all(pieces, "seq", 0, 0, axis_index_groups=groups)

    def by_position(moved, count):
        return jnp.transpose(moved, (1, 0, 2)).reshape(count, head_dim, GROUP * PIECE)

    item_ends = jnp.cumsum(short_lengths[0])
    positions = jnp.arange(short_rows, dtype=jnp.int32)
    item_ids = jnp.sum((positions[:, None] >= item_ends[None, :]).astype(jnp.int32), axis=1)
    ids_row = jnp.pad(item_ids, (REACH, REACH), constant_values=-1)[None, :]
    ids_col = item_ids[:, None]
    item_starts = jnp.concatenate([jnp.zeros((1,), jnp.int32), item_ends[:-1]])
    block_first = jnp.arange(0, short_rows, PIECE, dtype=jnp.int32)
    block_last = block_first + (PIECE - 1)
    inside = (item_starts[None, :] <= block_last[:, None]) & (
        item_ends[None, :] > block_first[:, None]
    )
    lowest = jnp.min(jnp.where(inside, item_starts[None, :], short_rows), axis=1)
    highest = jnp.max(jnp.where(inside, item_ends[None, :], 0), axis=1)
    reach = jnp.stack([lowest // PIECE, (highest + PIECE - 1) // PIECE]).astype(jnp.int32)

    first_tap = REACH - HALF_WIDTH
    tap_pad = ((0, 0), (first_tap, PIECE + 2 * REACH - first_tap - CONV_WIDTH))
    lines = jnp.pad(conv_kernel, tap_pad)[:, None, :]
    lines_back = jnp.pad(conv_kernel[:, ::-1], tap_pad)[:, None, :]
    unit_head = place % heads_dev
    long_line = lax.dynamic_index_in_dim(lines, unit_head, 0, False)
    long_line_back = lax.dynamic_index_in_dim(lines_back, unit_head, 0, False)

    long_send, short_pack, unit, inverse = project_in(
        tokens, query_weight, key_weight, value_weight, heads_dev
    )
    long_moved = exchange(long_send)
    short_att, short_w, short_s = short_forward(reach, ids_row, ids_col, short_pack, lines)
    long_moved, short_att = after(long_moved, short_att)
    long_pack = by_position(long_moved, 3)
    long_att, long_w, long_s = long_forward(long_pack[0], long_pack[1], long_pack[2], long_line)
    mixed, proj_own = project_out(exchange(long_att), short_att, out_weight)

    gain_one, bias_one, gain_two, bias_two = (
        line[None, :] for line in (gain_one, bias_one, gain_two, bias_two)
    )
    norm_unit, norm_inverse, normed_low, act_low, act_slope, ffn_own = feed_forward(
        tokens, proj_own, other_half(proj_own), gain_one, bias_one, inner_weight, outer_weight
    )
    output, grad_sum, grad_ffn_low, grad_pre_low, back_own, gain_two_grad, bias_two_grad = (
        feed_back(
            norm_unit, ffn_own, other_half(ffn_own), gain_one, bias_one, gain_two, bias_two,
            cotangent, act_slope, inner_weight, outer_weight,
        )
    )
    grad_hidden, grad_proj_low, long_grad, short_grad, gain_one_grad, bias_one_grad = project_back(
        norm_unit, norm_inverse, grad_sum, back_own, other_half(back_own), gain_one, out_weight,
        heads_dev,
    )

    long_grad = exchange(long_grad)
    outer_grad = contract(act_low, grad_ffn_low, 0, 0)
    inner_grad = contract(normed_low, grad_pre_low, 0, 0)
    out_grad = contract(mixed, grad_proj_low, 1, 0)
    peers = lax.axis_size("seq")
    every_bit = list(range(peers.bit_length() - 1))[::-1]
    orders = [[0, 1] + every_bit[:-2], [1, 0] + every_bit[:-2], [1, 0] + every_bit[:-2]]
    left = [list(every_bit) for _ in orders]
    parts = [
        grad.astype(BF16).reshape([2] * len(every_bit) + [-1, grad.shape[1]])
        for grad in (outer_grad, inner_grad, out_grad)
    ]

    def split(turn):
        return [halves(part, has, order[turn]) for part, has, order in zip(parts, left, orders)]

    def join(pairs, turn):
        for has, order in zip(left, orders):
            has.remove(order[turn])
        return [across_bit(*pair, order[turn]) for pair, order in zip(pairs, orders)]

    def short_half(half, grad):
        return short_backward(
            half, 2, reach, ids_row, ids_col, short_pack, grad, lines_back, short_w, short_s
        )

    pairs, short_grad = after(split(0), short_grad)
    *short_first, first_taps = short_half(0, short_grad)
    long_grad, short_first = after(long_grad, short_first)
    long_grad = by_position(long_grad, 1)[0]
    long_dv, long_taps = long_back_values(long_pack[2], long_grad, long_line_back, long_w)
    parts = join(pairs, 0)
    pairs, long_dv, long_grad = lax.optimization_barrier((split(1), long_dv, long_grad))
    norm_lines = jnp.concatenate(
        [gain_one_grad, bias_one_grad, gain_two_grad, bias_two_grad], axis=0
    ).reshape(-1, PIECE)
    norm_count = norm_lines.shape[0]
    norm_lines = jnp.pad(norm_lines, ((0, 16 - norm_count), (0, 0))).astype(BF16)
    long_dv = exchange(
        jnp.concatenate([long_dv, jnp.broadcast_to(norm_lines[None], (GROUP, 16, PIECE))], axis=1)
    )
    long_dq, long_dk = long_back_pairs(
        long_pack[0], long_pack[1], long_pack[2], long_grad, long_s
    )
    parts = join(pairs, 1)
    pairs, long_dv, long_dq, short_grad = lax.optimization_barrier(
        (split(2), long_dv, long_dq, short_grad)
    )
    *short_last, last_taps = short_half(1, short_grad)
    short_taps = jnp.concatenate([first_taps, last_taps], axis=0)
    long_back = exchange(jnp.concatenate([long_dq, long_dk], axis=1))
    parts = join(pairs, 2)
    for turn in range(3, len(every_bit)):
        parts = join(split(turn), turn)
    norm_sums = jnp.sum(long_dv[:, head_dim : head_dim + norm_count].astype(F32), axis=0)
    norm_sums = norm_sums.reshape(4, width)
    taps = slice(first_tap, first_tap + CONV_WIDTH)
    owner = (jnp.arange(heads_dev) == unit_head) & (place < units)
    kernel_part = short_taps[:, 0, taps] + jnp.where(owner[:, None], long_taps[:, taps], 0.0)
    if len(groups) > 1:
        same_place = [list(pick) for pick in zip(*groups)]
        norm_sums = lax.psum(norm_sums, "seq", axis_index_groups=same_place)
    parts, long_back, short_last = lax.optimization_barrier((parts, long_back, short_last))
    outer_part, inner_part, out_part = parts
    joined = jnp.concatenate(
        [outer_part, inner_part[:, :width], inner_part[:, width:], out_part], axis=0
    )
    joined = lax.all_gather(joined, "seq", axis=0)
    grads_low = unit_back(long_back, long_dv, [short_first, short_last], unit, inverse)
    weight_part = contract(tokens, grads_low, 0, 1).astype(BF16).reshape(peers, -1, 3 * head_cols)
    taps_line = kernel_part.reshape(1, 1, -1).astype(BF16)
    taps_line = jnp.pad(taps_line, ((0, 0), (0, 15), (0, 3 * head_cols - taps_line.shape[2])))
    weight_pieces = lax.all_to_all(
        jnp.concatenate([weight_part, jnp.broadcast_to(taps_line, (peers, 16, 3 * head_cols))], axis=1),
        "seq", 0, 0,
    )
    weight_all = jnp.concatenate([query_weight, key_weight, value_weight], axis=1)
    token_own = contract(grads_low, weight_all, 0, 1).astype(BF16)
    weight_pieces, token_own, joined = lax.optimization_barrier((weight_pieces, token_own, joined))
    joined = joined.astype(F32)
    marks = [outer_part.shape[0]]
    marks += [marks[0] + inner_part.shape[0], marks[0] + 2 * inner_part.shape[0]]
    outer_sum = joined[:, : marks[0]].reshape(outer_weight.shape)
    inner_sum = jnp.concatenate(
        [joined[:, marks[0] : marks[1]], joined[:, marks[1] : marks[2]]], axis=2
    ).reshape(inner_weight.shape)
    out_sum = joined[:, marks[2] :].reshape(out_weight.shape)
    pieces = jnp.sum(weight_pieces.astype(F32), axis=0)
    own_rows = weight_part.shape[1]
    kernel_sum = pieces[own_rows, : heads_dev * CONV_WIDTH].reshape(heads_dev, CONV_WIDTH)
    weight_sum = lax.all_gather(pieces[:own_rows].astype(BF16), "seq", axis=0, tiled=True)
    token_grad = grad_hidden + (token_own.astype(F32) + other_half(token_own).astype(F32))
    return (
        output,
        token_grad,
        weight_sum[:, :head_cols].astype(F32),
        weight_sum[:, head_cols : 2 * head_cols].astype(F32),
        weight_sum[:, 2 * head_cols :].astype(F32),
        kernel_sum,
        out_sum,
        norm_sums[0],
        norm_sums[1],
        inner_sum,
        outer_sum,
        norm_sums[2],
        norm_sums[3],
    )


def solution(mesh):
    rows = P("seq", None)
    columns = P(None, "tp")
    split_rows = P("tp", None)
    return jax.shard_map(
        shards,
        mesh=mesh,
        in_specs=(
            rows, rows, columns, columns, columns, split_rows, split_rows,
            P(), P(), columns, split_rows, P(), P(), rows,
        ),
        out_specs=(
            rows, rows, columns, columns, columns, split_rows, split_rows,
            P(), P(), columns, split_rows, P(), P(),
        ),
        check_vma=False,
    )
```

time: 785 us -> 626 us (0.80)
  blocking collectives: 136 us -> 29.2 us
  local copies, waits for them, and re-layouts: 141 us -> 35 us
  Pallas kernels: 176 us -> 262 us
  matrix products: 86.2 us -> 27.2 us
  waiting for transfers between devices: 130 us -> 177 us
  other arithmetic: 56.2 us -> 21.5 us
  starting transfers between devices: 36.5 us -> 49.2 us
    psum x1 -> x0, blocking collectives: 105 us -> none  [shards(): lax.psum((kernel_grad, gain_one_grad, bias_one_grad, gain_two_grad, bias_...]
    pallas_call x1 -> x8, Pallas kernels: 49.2 us -> 129 us  [the longest x1 32.1 us: long_back_pairs(): pl.pallas_call(body, grid=(blocks,), in_specs=[piece, whole, whole, piece...]
    all_gather x2, waiting for transfers between devices: 0.01 us -> 75.4 us  [the longest x1 40 us: shards(): lax.all_gather(pieces[:own_rows].astype(BF16), 'seq', axis=0, tiled=True)]
    all_to_all x5, waiting for transfers between devices: 120 us -> 56.6 us  [the longest x1 54.8 us: shards(): lax.all_to_all(jnp.concatenate([weight_part, jnp.broadcast_to(taps_line,...]
    reshape x15 -> x1, local copies, waits for them, and re-layouts: 35 us -> 0.01 us  [shards(): norm_lines = jnp.concatenate([gain_one_grad, bias_one_grad, gain_two_grad...]
    ppermute x4 -> x16, waiting for transfers between devices: 10 us -> 44.8 us  [the longest x12 37.8 us: across_bit(): came = lax.ppermute(sent, 'seq', [(i, i ^ 1 << bit) for i in range(peers)])]
    dot_general x2 -> x0, matrix products: 30.2 us -> none  [the longest x1 25.2 us: shards(): pre_act = jnp.dot(normed_low, inner_weight, preferred_element_type=F32)]
    reduce_sum x13 -> x2, other arithmetic: 31.4 us -> 1.26 us  [the longest x1 0.94 us: shards(): jnp.sum(long_dv[:, head_dim:head_dim + norm_count].astype(F32), axis=0)]
  transfers between devices with their start and end apart: 11 -> 23, of which waited for: 6 -> 11; matrix products, arithmetic and copies ran while one was open for 17% -> 10% of each run, Pallas kernels for 7% -> 20%
where the time goes in v2:
time: 626 us; the launch traced here: 616 us
  Pallas kernels  262 us (42%)
  waiting for transfers between devices  177 us (28%)
  starting transfers between devices  49.2 us (8%)
  local copies, waits for them, and re-layouts  35 us (6%)
  blocking collectives  29.2 us (5%)
  matrix products  27.2 us (4%)
  other arithmetic  21.5 us (3%)
  between operations  14.9 us (2%)
    pallas_call x1, Pallas kernels, long_forward(): pl.pallas_call(body, grid=(blocks,), in_specs=[pl.BlockSpec((head_dim, PI...  71.9 us
    all_to_all x1, waiting for transfers between devices, shards(): lax.all_to_all(jnp.concatenate([weight_part, jnp.broadcast_to(taps_line,...  54.8 us
    all_gather x1, waiting for transfers between devices, shards(): lax.all_gather(pieces[:own_rows].astype(BF16), 'seq', axis=0, tiled=True)  40 us
    ppermute x12, waiting for transfers between devices, across_bit(): came = lax.ppermute(sent, 'seq', [(i, i ^ 1 << bit) for i in range(peers)])  37.8 us
    all_gather x1, waiting for transfers between devices, shards(): joined = lax.all_gather(joined, 'seq', axis=0)  35.4 us
    pallas_call x2, Pallas kernels, short_backward(): pl.pallas_call(body, grid=(blocks,), in_specs=[pl.BlockSpec(memory_space=...  33 us
    pallas_call x1, Pallas kernels, long_back_pairs(): pl.pallas_call(body, grid=(blocks,), in_specs=[piece, whole, whole, piece...  32.1 us
    all_to_all x1, blocking collectives, exchange(): return lax.all_to_all(pieces, 'seq', 0, 0, axis_index_groups=groups)  29.2 us
  transfers between devices with their start and end apart: 23, of which 11 were waited for; matrix products, arithmetic and copies ran while one was open for 10% of the time, Pallas kernels for 20%

profile of v2, /device:TPU:0, one launch (start us, length us, event | category | flops | bytes accessed | tf_op | source)
XLA Modules:
  0.0 616.0 jit_solution(11048399179111554244)
XLA Ops:
  7.2 10.0 %shard_map.237 = (bf16[16,192,256]{2,1,0:T(8,128)(2,1)}, bf16[3,6,64,1024]{3,2,1,0:T(8,128)(2,1)}, f32[2,6,64,1536]{3,2,1,0:T(8,128)}, f32[2,6,1,1536]{3,2,1,0:T(1,128)}) custom-call(bf16[1536,768]{1,0:T(8,128)(2,1)} %t_ref.3, bf16[768,384]{1,0:T(8,128)(2,1)} %wq_ref.1, bf16[768,384]{1,0:T(8,128)(2,1)} %wk_ref.1, bf16[768,384]{1,0:T(8,128)(2,1)} %wv_ref.1), custom_call_target="tpu_custom_call" | custom-call | flops 11500000256 | tf_op jit(solution)/shard_map/pallas_call | solution.py:511
  17.2 8.5 %all-to-all-start = ((bf16[16,192,256]{2,1,0:T(8,128)(2,1)}), bf16[16,192,256]{2,1,0:T(8,128)(2,1)S(1)}, u32[]{:S(2)}, u32[]{:S(2)}) async-start(bf16[16,192,256]{2,1,0:T(8,128)(2,1)} %get-tuple-element.96), calls=%async_computation | async-start | bytes 3145728 | tf_op jit(solution)/shard_map/all_to_all | solution.py:883
  29.9 28.1 %shard_map.238 = (bf16[6,64,1024]{2,1,0:T(8,128)(2,1)}, bf16[4,6,1024,256]{3,2,1,0:T(8,128)(2,1)}, bf16[4,6,1024,256]{3,2,1,0:T(8,128)(2,1)}) custom-call(s32[2,4]{1,0:T(2,128)} %pad_add_fusion.reach_ref, s32[1,1280]{1,0:T(1,128)} %broadcast_in_dim.86.row_ref, s32[1024,1]{1,0:T(8,128)} %copy.40.col_ref, ...), custom_call_target="tpu_custom_call" | custom-call | flops 32199999488 | tf_op jit(solution)/shard_map/pallas_call | solution.py:338
  58.0 1.8 all-to-all-done
  62.4 71.9 %shard_map.239 = (bf16[16,64,256]{2,1,0:T(8,128)(2,1)}, bf16[16,4096,256]{2,1,0:T(8,128)(2,1)}, bf16[16,4096,256]{2,1,0:T(8,128)(2,1)}) custom-call(bf16[64,4096]{1,0:T(8,128)(2,1)} %bitcast.129, bf16[64,4096]{1,0:T(8,128)(2,1)} %bitcast.127, bf16[64,4096]{1,0:T(8,128)(2,1)} %bitcast.124, f32[1,512]{1,0:T(1,128)} %get-tuple-element.215.line_ref), custom_call_target="tpu_custom_call" | custom-call | flops 80499998720 | tf_op jit(solution)/shard_map/pallas_call | solution.py:150
  134.3 29.2 %all_to_all.30.m_ref = bf16[16,64,256]{2,1,0:T(8,128)(2,1)} all-to-all(bf16[16,64,256]{2,1,0:T(8,128)(2,1)} %get-tuple-element.100), channel_id=1, replica_groups={{0,2,4,6,8,10,12,14,16,18,20,22,24,26,28,30},{1,3,5,7,9,11,13,15,17,19,..., dimensions={0} | all-to-all | bytes 1048576 | tf_op jit(solution)/shard_map/all_to_all | solution.py:883
  163.5 5.2 shard_map.240
  169.9 3.6 collective-permute-done.other_ref
  174.9 19.8 %shard_map.241 = (f32[1536,768]{1,0:T(8,128)}, f32[1536,1]{1,0:T(8,128)}, bf16[1536,768]{1,0:T(8,128)(2,1)}, bf16[1536,1536]{1,0:T(8,128)(2,1)}, bf16[1536,1536]{1,0:T(8,128)(2,1)}, /*index=5*/bf16[1536,768]{1,0:T(8,128)(2,1)}) custom-call(bf16[1536,768]{1,0:T(8,128)(2,1)} %t_ref.3, bf16[1536,768]{1,0:T(8,128)(2,1)} %get-tuple-element.102.own_ref, ...), custom_call_target="tpu_custom_call" | custom-call | flops 23000000512 | tf_op jit(solution)/shard_map/pallas_call | solution.py:606
  196.1 3.4 collective-permute-done.1.other_ref
  200.9 17.7 %shard_map.242 = (bf16[1536,768]{1,0:T(8,128)(2,1)}, f32[1536,768]{1,0:T(8,128)}, bf16[1536,768]{1,0:T(8,128)(2,1)}, bf16[1536,1536]{1,0:T(8,128)(2,1)}, bf16[15...) custom-call(f32[1536,768]{1,0:T(8,128)} %get-tuple-element.103.unit_ref, ...), custom_call_target="tpu_custom_call" | custom-call | flops 20700000256 | tf_op jit(solution)/shard_map/pallas_call | solution.py:665
  220.9 7.1 %convolution_convert_fusion.3 = bf16[1536,768]{1,0:T(8,128)(2,1)S(1)} fusion(bf16[1536,1536]{1,0:T(8,128)(2,1)} %get-tuple-element.111, bf16[1536,768]{1,0:T(8,128)(2,1)} %get-tuple-element.112), kind=kOutput, calls=%fused_computation.6 | convolution fusion | flops 3625058304 | bytes 9437184 | tf_op jit(solution)/shard_map/dot_general | solution.py:66
  229.3 1.6 copy-done.22
  230.8 4.1 convolution_convert_fusion.2
  236.2 12.4 %shard_map.243 = (f32[1536,768]{1,0:T(8,128)}, bf16[1536,768]{1,0:T(8,128)(2,1)}, bf16[16,64,256]{2,1,0:T(8,128)(2,1)}, bf16[6,64,1024]{2,1,0:T(8,128)(2,1)}, f32[1,768]{1,0:T(1,128)}, /*index=5*/f32[1,768]{1,0:T(1,128)}) custom-call(f32[1536,768]{1,0:T(8,128)} %get-tuple-element.103.unit_ref, f32[1536,1]{1,0:T(8,128)} %get-tuple-element.107.inv_ref, ...), custom_call_target="tpu_custom_call" | custom-call | flops 13799999488 | tf_op jit(solution)/shard_map/pallas_call | solution.py:735
  248.6 3.1 convolution_convert_fusion.4
  252.5 3.9 all-to-all-start.2
  256.4 1.9 collective-permute-start.5
  260.4 16.6 %shard_map.244 = (f32[3,64,1024]{2,1,0:T(8,128)}, f32[3,64,1024]{2,1,0:T(8,128)}, f32[3,64,1024]{2,1,0:T(8,128)}, f32[3,1,512]{2,1,0:T(1,128)}) custom-call(s32[2,4]{1,0:T(2,128)} %pad_add_fusion.reach_ref, s32[1,1280]{1,0:T(1,128)} %broadcast_in_dim.86.row_ref, s32[1024,1]{1,0:T(8,128)} %copy.40.col_ref, ...), custom_call_target="tpu_custom_call" | custom-call | flops 32199999488 | tf_op jit(solution)/shard_map/pallas_call | solution.py:429
  278.0 23.7 %shard_map.245 = (bf16[16,64,256]{2,1,0:T(8,128)(2,1)}, f32[1,512]{1,0:T(1,128)}) custom-call(bf16[64,4096]{1,0:T(8,128)(2,1)} %bitcast.125, bf16[64,4096]{1,0:T(8,128)(2,1)} %bitcast.131, f32[1,512]{1,0:T(1,128)} %get-tuple-element.216.line_ref, bf16[16,4096,256]{2,1,0:T(8,128)(2,1)} %get-tuple-element.132.w_ref), custom_call_target="tpu_custom_call" | custom-call | flops 18400000000 | tf_op jit(solution)/shard_map/pallas_call | solution.py:207
  301.7 1.5 add_convert_fusion.1
  304.2 1.6 add_convert_fusion
  307.8 9.5 %all-to-all-start.3 = ((bf16[16,80,256]{2,1,0:T(8,128)(2,1)}), bf16[16,80,256]{2,1,0:T(8,128)(2,1)S(1)}, u32[]{:S(2)}, u32[]{:S(2)}) async-start(bf16[16,80,256]{2,1,0:T(8,128)(2,1)} %pad_maximum_fusion.3), calls=%async_computation.3 | async-start | bytes 1310720 | tf_op jit(solution)/shard_map/all_to_all | solution.py:883
  317.3 2.1 collective-permute-start.6
  320.8 32.1 %shard_map.246 = (bf16[16,64,256]{2,1,0:T(8,128)(2,1)}, bf16[16,64,256]{2,1,0:T(8,128)(2,1)}) custom-call(bf16[64,4096]{1,0:T(8,128)(2,1)} %bitcast.130, bf16[64,4096]{1,0:T(8,128)(2,1)} %bitcast.128, bf16[64,4096]{1,0:T(8,128)(2,1)} %bitcast.126, bf16[64,4096]{1,0:T(8,128)(2,1)} %bitcast.132, bf16[16,4096,256]{2,1,0:T(8,128)(2,1)} %get-tuple-element.146.s_ref), custom_call_target="tpu_custom_call" | custom-call | flops 46000001024 | tf_op jit(solution)/shard_map/pallas_call | solution.py:268
  354.2 2.4 collective-permute-start.13
  356.6 16.5 %shard_map.247 = (f32[3,64,1024]{2,1,0:T(8,128)}, f32[3,64,1024]{2,1,0:T(8,128)}, f32[3,64,1024]{2,1,0:T(8,128)}, f32[3,1,512]{2,1,0:T(1,128)}) custom-call(s32[2,4]{1,0:T(2,128)} %pad_add_fusion.reach_ref, s32[1,1280]{1,0:T(1,128)} %broadcast_in_dim.86.row_ref, s32[1024,1]{1,0:T(8,128)} %copy.40.col_ref, ...), custom_call_target="tpu_custom_call" | custom-call | flops 32199999488 | tf_op jit(solution)/shard_map/pallas_call | solution.py:429
  373.1 3.9 collective-permute-start.9
  378.7 5.3 all-to-all-start.4
  384.1 7.8 %collective-permute-done.14 = bf16[24,768]{1,0:T(8,128)(2,1)S(1)} collective-permute-done((bf16[24,768]{1,0:T(8,128)(2,1)S(1)}, bf16[24,768]{1,0:T(8,128)(2,1)S(1)}, u32[]{:S(2)}, u32[]{:S(2)}) %collective-permute-start.14) | collective-permute-done | bytes 36896 | tf_op jit(solution)/shard_map/ppermute | solution.py:847
  391.9 13.5 %collective-permute-done.9 = bf16[2,96,768]{2,1,0:T(8,128)(2,1)S(1)} collective-permute-done((bf16[2,96,768]{2,1,0:T(8,128)(2,1)}, bf16[2,96,768]{2,1,0:T(8,128)(2,1)S(1)}, u32[]{:S(2)}, u32[]{:S(2)}) %collective-permute-start.9) | collective-permute-done | bytes 294944 | tf_op jit(solution)/shard_map/ppermute | solution.py:847
  405.5 6.2 %collective-permute-done.11 = bf16[2,48,1536]{2,1,0:T(8,128)(2,1)S(1)} collective-permute-done((bf16[2,48,1536]{2,1,0:T(8,128)(2,1)S(1)}, bf16[2,48,1536]{2,1,0:T(8,128)(2,1)S(1)}, u32[]{:S(2)}, u32[]{:S(2)}) %collective-permute-start.11) | collective-permute-done | bytes 294944 | tf_op jit(solution)/shard_map/ppermute | solution.py:847
  413.2 7.3 %collective-permute-done.10 = bf16[96,768]{1,0:T(8,128)(2,1)S(1)} collective-permute-done((bf16[96,768]{1,0:T(8,128)(2,1)S(1)}, bf16[96,768]{1,0:T(8,128)(2,1)S(1)}, u32[]{:S(2)}, u32[]{:S(2)}) %collective-permute-start.10) | collective-permute-done | bytes 147488 | tf_op jit(solution)/shard_map/ppermute | solution.py:847
  420.5 3.0 collective-permute-done.12
  425.5 7.9 %shard_map.248 = bf16[1152,1536]{1,0:T(8,128)(2,1)} custom-call(bf16[16,128,256]{2,1,0:T(8,128)(2,1)} %copy-done.1, bf16[16,80,256]{2,1,0:T(8,128)(2,1)} %copy-done.2, f32[3,64,1024]{2,1,0:T(8,128)} %get-tuple-element.162.refs_2_, f32[3,64,1024]{2,1,0:T(8,128)} %get-tuple-element.163.refs_3_, f32[3,64,1024]{2,1,0:T(8,128)} %get-tuple-element.164.refs_4_, ...), custom_call_target="tpu_custom_call" | custom-call | flops 9200000000 | tf_op jit(solution)/shard_map/pallas_call | solution.py:813
  433.5 6.0 convolution_convert_fusion.1
  439.6 1.7 pad_maximum_fusion.1
  441.3 5.3 all-to-all-start.5
  446.9 6.8 %convolution_convert_fusion = bf16[1536,768]{1,0:T(8,128)(2,1)} fusion(bf16[1152,1536]{1,0:T(8,128)(2,1)} %shard_map.248, bf16[768,384]{1,0:T(8,128)(2,1)} %wv_ref.1, bf16[768,384]{1,0:T(8,128)(2,1)S(1)} %copy-done.20, bf16[768,384]{1,0:T(8,128)(2,1)S(1)} %copy-done.19), kind=kOutput, calls=%fused_computation.3 | convolution fusion | flops 2724397056 | bytes 7667712 | tf_op jit(solution)/shard_map/dot_general | solution.py:66
  453.8 54.8 %all-to-all-done.5 = bf16[16,64,1152]{2,1,0:T(8,128)(2,1)S(1)} async-done(((bf16[16,64,1152]{2,1,0:T(8,128)(2,1)}), bf16[16,64,1152]{2,1,0:T(8,128)(2,1)S(1)}, u32[]{:S(2)}, u32[]{:S(2)}) %all-to-all-start.5) | async-done | bytes 2359328 | tf_op jit(solution)/shard_map/all_to_all | solution.py:1010
  508.6 35.4 %all-gather.6.cloned.1.call-done = bf16[3456,768]{1,0:T(8,128)(2,1)} async-done(((bf16[216,768]{1,0:T(8,128)(2,1)}), bf16[3456,768]{1,0:T(8,128)(2,1)}) %all-gather.6.cloned.1.call-update) | async-done | bytes 5308432 | tf_op jit(solution)/shard_map/all_gather | solution.py:1005
  548.4 2.2 slice.112
  550.6 4.3 slice.117
  555.6 2.2 fusion.10
  557.9 3.1 pad_maximum_fusion
  562.7 2.9 add_add_fusion
  565.6 40.0 %all-gather.4.cloned.1.call-done = bf16[768,1152]{1,0:T(8,128)(2,1)} async-done(((bf16[48,1152]{1,0:T(8,128)(2,1)}), bf16[768,1152]{1,0:T(8,128)(2,1)}) %all-gather.4.cloned.1.call-update) | async-done | bytes 1769488 | tf_op jit(solution)/shard_map/all_gather | solution.py:1028
  605.6 3.3 slice_convert_fusion
  (160 shorter events, 38.6 us)
Async XLA Ops:
  17.1 8.5 %copy-start.6 = (f32[6,33]{1,0:T(8,128)S(1)}, f32[6,33]{1,0:T(8,128)}, u32[]{:S(2)}) copy-start(f32[6,33]{1,0:T(8,128)} %param.19) | copy-start | bytes 2380
  17.1 8.7 %copy-start.21 = (s32[1,3]{1,0:T(1,128)S(1)}, s32[1,3]{1,0:T(1,128)}, u32[]{:S(2)}) copy-start(s32[1,3]{1,0:T(1,128)} %param.15) | copy-start | bytes 40
  17.2 42.6 %all-to-all-start = ((bf16[16,192,256]{2,1,0:T(8,128)(2,1)}), bf16[16,192,256]{2,1,0:T(8,128)(2,1)S(1)}, u32[]{:S(2)}, u32[]{:S(2)}) async-start(bf16[16,192,256]{2,1,0:T(8,128)(2,1)} %get-tuple-element.96), calls=%async_computation | async-start | bytes 3145728 | tf_op jit(solution)/shard_map/all_to_all | solution.py:883
  25.8 32.2 %copy-start.7 = (f32[6,33]{1,0:T(8,128)}, f32[6,33]{1,0:T(8,128)S(1)}, u32[]{:S(2)}) copy-start(f32[6,33]{1,0:T(8,128)S(1)} %rev.3) | copy-start | bytes 2380
  163.5 5.2 copy-start.11
  163.5 5.8 copy-start.12
  168.7 4.7 collective-permute-start
  169.9 25.0 %copy-start.13 = (f32[768]{0:T(1024)S(1)}, f32[768]{0:T(1024)}, u32[]{:S(2)}) copy-start(f32[768]{0:T(1024)} %param.25) | copy-start | bytes 9220
  169.9 25.6 %copy-start.14 = (f32[768]{0:T(1024)S(1)}, f32[768]{0:T(1024)}, u32[]{:S(2)}) copy-start(f32[768]{0:T(1024)} %param.26) | copy-start | bytes 9220
  173.5 1.4 copy-start.18
  194.8 4.8 collective-permute-start.1
  200.9 17.9 %copy-start.8 = (f32[6,33]{1,0:T(8,128)S(1)}, f32[6,33]{1,0:T(8,128)}, u32[]{:S(2)}) copy-start(f32[6,33]{1,0:T(8,128)} %copy-done.7) | copy-start | bytes 2380
  218.7 17.6 %collective-permute-start.2 = (bf16[1536,768]{1,0:T(8,128)(2,1)}, bf16[1536,768]{1,0:T(8,128)(2,1)}, u32[]{:S(2)}, u32[]{:S(2)}) collective-permute-start(bf16[1536,768]{1,0:T(8,128)(2,1)} %get-tuple-element.109.own_ref), channel_id=1, source_target_pairs={{0,1},{1,0},{2,3},{3,2},{4,5},{5,4},{6,7},{7,6},{8,9},{9,8},{10,11... | collective-permute-start | bytes 7077896 | tf_op jit(solution)/shard_map/ppermute | solution.py:834
  220.9 8.3 %copy-start.23 = (bf16[1536,768]{1,0:T(8,128)(2,1)S(1)}, bf16[1536,768]{1,0:T(8,128)(2,1)}, u32[]{:S(2)}) copy-start(bf16[1536,768]{1,0:T(8,128)(2,1)} %get-tuple-element.113) | copy-start | bytes 7077892
  228.1 2.8 copy-start.22
  252.5 24.7 %all-to-all-start.2 = ((bf16[16,64,256]{2,1,0:T(8,128)(2,1)}), bf16[16,64,256]{2,1,0:T(8,128)(2,1)S(1)}, u32[]{:S(2)}, u32[]{:S(2)}) async-start(bf16[16,64,256]{2,1,0:T(8,128)(2,1)} %get-tuple-element.124), calls=%async_computation.2 | async-start | bytes 1048576 | tf_op jit(solution)/shard_map/all_to_all | solution.py:883
  256.4 20.6 %collective-permute-start.5 = (bf16[2,2,2,24,768]{4,3,2,1,0:T(8,128)(2,1)}, bf16[2,2,2,24,768]{4,3,2,1,0:T(8,128)(2,1)S(1)}, u32[]{:S(2)}, u32[]{:S(2)}) collective-permute-start(bf16[2,2,2,24,768]{4,3,2,1,0:T(8,128)(2,1)} %get-tuple-element.123), channel_id=1, source_target_pairs={{0,4},{2,6},{4,0},{6,2},{8,12},{10,14},{12,8},{14,10},{16,20},{18,... | collective-permute-start | bytes 884744 | tf_op jit(solution)/shard_map/ppermute | solution.py:847
  258.3 43.4 %collective-permute-start.3 = (bf16[2,2,2,96,768]{4,3,2,1,0:T(8,128)(2,1)}, bf16[2,2,2,96,768]{4,3,2,1,0:T(8,128)(2,1)}, u32[]{:S(2)}, u32[]{:S(2)}) collective-permute-start(bf16[2,2,2,96,768]{4,3,2,1,0:T(8,128)(2,1)} %get-tuple-element.119), channel_id=1, source_target_pairs={{0,2},{2,0},{4,6},{6,4},{8,10},{10,8},{12,14},{14,12},{16,18},{18,... | collective-permute-start | bytes 3538952 | tf_op jit(solution)/shard_map/ppermute | solution.py:847
  259.8 44.4 %collective-permute-start.4 = (bf16[2,2,2,48,1536]{4,3,2,1,0:T(8,128)(2,1)}, bf16[2,2,2,48,1536]{4,3,2,1,0:T(8,128)(2,1)}, u32[]{:S(2)}, u32[]{:S(2)}) collective-permute-start(bf16[2,2,2,48,1536]{4,3,2,1,0:T(8,128)(2,1)} %get-tuple-element.121), channel_id=1, source_target_pairs={{0,4},{2,6},{4,0},{6,2},{8,12},{10,14},{12,8},{14,10},{16,20},{18,... | collective-permute-start | bytes 3538952 | tf_op jit(solution)/shard_map/ppermute | solution.py:847
  260.4 16.6 %copy-start.16 = (f32[1,768]{1,0:T(1,128)S(1)}, f32[1,768]{1,0:T(1,128)}, u32[]{:S(2)}) copy-start(f32[1,768]{1,0:T(1,128)} %get-tuple-element.141) | copy-start | bytes 9220
  260.4 16.6 %copy-start.15 = (f32[1,768]{1,0:T(1,128)S(1)}, f32[1,768]{1,0:T(1,128)}, u32[]{:S(2)}) copy-start(f32[1,768]{1,0:T(1,128)} %get-tuple-element.142) | copy-start | bytes 9220
  304.2 2.7 copy-start.3
  306.7 46.2 %collective-permute-start.8 = (bf16[2,2,24,768]{3,2,1,0:T(8,128)(2,1)S(1)}, bf16[2,2,24,768]{3,2,1,0:T(8,128)(2,1)S(1)}, u32[]{:S(2)}, u32[]{:S(2)}) collective-permute-start(bf16[2,2,24,768]{3,2,1,0:T(8,128)(2,1)S(1)} %get-tuple-element.139), channel_id=1, source_target_pairs={{0,2},{2,0},{4,6},{6,4},{8,10},{10,8},{12,14},{14,12},{16,18},{18,... | collective-permute-start | bytes 442376 | tf_op jit(solution)/shard_map/ppermute | solution.py:847
  307.8 46.4 %all-to-all-start.3 = ((bf16[16,80,256]{2,1,0:T(8,128)(2,1)}), bf16[16,80,256]{2,1,0:T(8,128)(2,1)S(1)}, u32[]{:S(2)}, u32[]{:S(2)}) async-start(bf16[16,80,256]{2,1,0:T(8,128)(2,1)} %pad_maximum_fusion.3), calls=%async_computation.3 | async-start | bytes 1310720 | tf_op jit(solution)/shard_map/all_to_all | solution.py:883
  317.3 35.8 %collective-permute-start.6 = (bf16[2,2,96,768]{3,2,1,0:T(8,128)(2,1)}, bf16[2,2,96,768]{3,2,1,0:T(8,128)(2,1)S(1)}, u32[]{:S(2)}, u32[]{:S(2)}) collective-permute-start(bf16[2,2,96,768]{3,2,1,0:T(8,128)(2,1)} %get-tuple-element.135), channel_id=1, source_target_pairs={{0,4},{2,6},{4,0},{6,2},{8,12},{10,14},{12,8},{14,10},{16,20},{18,... | collective-permute-start | bytes 1769480 | tf_op jit(solution)/shard_map/ppermute | solution.py:847
  319.4 34.6 %collective-permute-start.7 = (bf16[2,2,48,1536]{3,2,1,0:T(8,128)(2,1)}, bf16[2,2,48,1536]{3,2,1,0:T(8,128)(2,1)S(1)}, u32[]{:S(2)}, u32[]{:S(2)}) collective-permute-start(bf16[2,2,48,1536]{3,2,1,0:T(8,128)(2,1)} %get-tuple-element.137), channel_id=1, source_target_pairs={{0,2},{2,0},{4,6},{6,4},{8,10},{10,8},{12,14},{14,12},{16,18},{18,... | collective-permute-start | bytes 1769480 | tf_op jit(solution)/shard_map/ppermute | solution.py:847
  354.2 18.9 %copy-start.2 = (bf16[16,80,256]{2,1,0:T(8,128)(2,1)}, bf16[16,80,256]{2,1,0:T(8,128)(2,1)S(1)}, u32[]{:S(2)}) copy-start(bf16[16,80,256]{2,1,0:T(8,128)(2,1)S(1)} %all-to-all-done.3.refs_1_) | copy-start | bytes 1966084
  354.2 23.5 %copy-start.4 = (bf16[16,64,256]{2,1,0:T(8,128)(2,1)S(1)}, bf16[16,64,256]{2,1,0:T(8,128)(2,1)}, u32[]{:S(2)}) copy-start(bf16[16,64,256]{2,1,0:T(8,128)(2,1)} %get-tuple-element.154) | copy-start | bytes 1572868
  354.2 23.5 %copy-start.5 = (bf16[16,64,256]{2,1,0:T(8,128)(2,1)S(1)}, bf16[16,64,256]{2,1,0:T(8,128)(2,1)}, u32[]{:S(2)}) copy-start(bf16[16,64,256]{2,1,0:T(8,128)(2,1)} %get-tuple-element.155) | copy-start | bytes 1572868
  354.2 22.9 %collective-permute-start.13 = (bf16[2,24,768]{2,1,0:T(8,128)(2,1)S(1)}, bf16[2,24,768]{2,1,0:T(8,128)(2,1)S(1)}, u32[]{:S(2)}, u32[]{:S(2)}) collective-permute-start(bf16[2,24,768]{2,1,0:T(8,128)(2,1)S(1)} %get-tuple-element.153), channel_id=1, source_target_pairs={{0,16},{2,18},{4,20},{6,22},{8,24},{10,26},{12,28},{14,30},{16,0},... | collective-permute-start | bytes 221192 | tf_op jit(solution)/shard_map/ppermute | solution.py:847
  373.1 32.2 %collective-permute-start.9 = (bf16[2,96,768]{2,1,0:T(8,128)(2,1)}, bf16[2,96,768]{2,1,0:T(8,128)(2,1)S(1)}, u32[]{:S(2)}, u32[]{:S(2)}) collective-permute-start(bf16[2,96,768]{2,1,0:T(8,128)(2,1)} %get-tuple-element.149), channel_id=1, source_target_pairs={{0,16},{2,18},{4,20},{6,22},{8,24},{10,26},{12,28},{14,30},{16,0},... | collective-permute-start | bytes 884744 | tf_op jit(solution)/shard_map/ppermute | solution.py:847
  377.1 34.7 %collective-permute-start.11 = (bf16[2,48,1536]{2,1,0:T(8,128)(2,1)S(1)}, bf16[2,48,1536]{2,1,0:T(8,128)(2,1)S(1)}, u32[]{:S(2)}, u32[]{:S(2)}) collective-permute-start(bf16[2,48,1536]{2,1,0:T(8,128)(2,1)S(1)} %get-tuple-element.151), channel_id=1, source_target_pairs={{0,16},{2,18},{4,20},{6,22},{8,24},{10,26},{12,28},{14,30},{16,0},... | collective-permute-start | bytes 884744 | tf_op jit(solution)/shard_map/ppermute | solution.py:847
  377.2 14.7 %collective-permute-start.14 = (bf16[24,768]{1,0:T(8,128)(2,1)S(1)}, bf16[24,768]{1,0:T(8,128)(2,1)S(1)}, u32[]{:S(2)}, u32[]{:S(2)}) collective-permute-start(bf16[24,768]{1,0:T(8,128)(2,1)S(1)} %dynamic-slice_bitcast_fusion.20), channel_id=1, source_target_pairs={{0,8},{2,10},{4,12},{6,14},{8,0},{10,2},{12,4},{14,6},{16,24},{18,... | collective-permute-start | bytes 110600 | tf_op jit(solution)/shard_map/ppermute | solution.py:847
  378.7 44.8 %all-to-all-start.4 = ((bf16[16,128,256]{2,1,0:T(8,128)(2,1)}), bf16[16,128,256]{2,1,0:T(8,128)(2,1)S(1)}, u32[]{:S(2)}, u32[]{:S(2)}) async-start(bf16[16,128,256]{2,1,0:T(8,128)(2,1)} %pad_maximum_fusion.2), calls=%async_computation.4 | async-start | bytes 2097152 | tf_op jit(solution)/shard_map/all_to_all | solution.py:883
  384.0 41.3 %copy-start.9 = (f32[3,1,512]{2,1,0:T(1,128)S(1)}, f32[3,1,512]{2,1,0:T(1,128)}, u32[]{:S(2)}) copy-start(f32[3,1,512]{2,1,0:T(1,128)} %get-tuple-element.170) | copy-start | bytes 18436
  384.0 41.3 %copy-start.10 = (f32[3,1,512]{2,1,0:T(1,128)S(1)}, f32[3,1,512]{2,1,0:T(1,128)}, u32[]{:S(2)}) copy-start(f32[3,1,512]{2,1,0:T(1,128)} %get-tuple-element.171) | copy-start | bytes 18436
  384.0 159.9 %all-gather.6.cloned.1.call-start = ((), (), s32[]{:S(2)}) async-start(), calls=%async_computation.7 | async-start | bytes 5640192 | tf_op jit(solution)/shard_map/all_gather | solution.py:1005
  405.4 15.0 %collective-permute-start.10 = (bf16[96,768]{1,0:T(8,128)(2,1)S(1)}, bf16[96,768]{1,0:T(8,128)(2,1)S(1)}, u32[]{:S(2)}, u32[]{:S(2)}) collective-permute-start(bf16[96,768]{1,0:T(8,128)(2,1)S(1)} %dynamic-slice_bitcast_fusion.15), channel_id=1, source_target_pairs={{0,8},{2,10},{4,12},{6,14},{8,0},{10,2},{12,4},{14,6},{16,24},{18,... | collective-permute-start | bytes 442376 | tf_op jit(solution)/shard_map/ppermute | solution.py:847
  411.9 11.6 %collective-permute-start.12 = (bf16[48,1536]{1,0:T(8,128)(2,1)S(1)}, bf16[48,1536]{1,0:T(8,128)(2,1)S(1)}, u32[]{:S(2)}, u32[]{:S(2)}) collective-permute-start(bf16[48,1536]{1,0:T(8,128)(2,1)S(1)} %dynamic-slice_bitcast_fusion.14), channel_id=1, source_target_pairs={{0,8},{2,10},{4,12},{6,14},{8,0},{10,2},{12,4},{14,6},{16,24},{18,... | collective-permute-start | bytes 442376 | tf_op jit(solution)/shard_map/ppermute | solution.py:847
  423.6 2.0 copy-start.1
  441.3 5.6 copy-start.19
  441.3 5.6 copy-start.20
  441.3 67.3 %all-to-all-start.5 = ((bf16[16,64,1152]{2,1,0:T(8,128)(2,1)}), bf16[16,64,1152]{2,1,0:T(8,128)(2,1)S(1)}, u32[]{:S(2)}, u32[]{:S(2)}) async-start(bf16[16,64,1152]{2,1,0:T(8,128)(2,1)} %pad_maximum_fusion.1), calls=%async_computation.5 | async-start | bytes 4718592 | tf_op jit(solution)/shard_map/all_to_all | solution.py:1010
  446.6 159.0 %all-gather.4.cloned.1.call-start = ((), (), s32[]{:S(2)}) async-start(), calls=%async_computation.6 | async-start | bytes 1880064 | tf_op jit(solution)/shard_map/all_gather | solution.py:1028
  545.0 16.0 %collective-permute-start.15 = (bf16[1536,768]{1,0:T(8,128)(2,1)}, bf16[1536,768]{1,0:T(8,128)(2,1)S(1)}, u32[]{:S(2)}, u32[]{:S(2)}) collective-permute-start(bf16[1536,768]{1,0:T(8,128)(2,1)} %convolution_convert_fusion), channel_id=1, source_target_pairs={{0,1},{1,0},{2,3},{3,2},{4,5},{5,4},{6,7},{7,6},{8,9},{9,8},{10,11... | collective-permute-start | bytes 7077896 | tf_op jit(solution)/shard_map/ppermute | solution.py:834
  557.8 3.5 slice-start
  557.8 3.9 slice-start.1
  557.9 4.8 copy-start
  (1 other events, 1.4 us)
Sparse Core Ops, SparseCore 0:
  424.5 119.3 all-gather.5
  547.3 58.2 all-gather.3
